TPU v7x, 32 devices: a whole 2x2x4 slice. The times are simulated.
32 devices in a mesh: gz: 2 (over y), gy: 4 (over x, core), gx: 4 (over z).
Axes of the slice: x: 2, y: 2, z: 4, core: 2. Of those that a mesh axis runs over, the one named last changes fastest.
Arguments:
- labels: int32 [2, 32, 512], P('gz', 'gy', 'gx'), may hold values from 0 to 7
- tissue_tensors: float32 [6, 8], replicated, as said below
- electrodes: int32 [2, 64], replicated, may hold values from 0 to 32767, as said below
- initial: float32 [64, 2, 32, 512], P(None, 'gz', 'gy', 'gx'), may hold values from -4 to 4
Outputs:
- solution: float32 [64, 2, 32, 512], P(None, 'gz', 'gy', 'gx')
- residual: float32 [64, 2, 32, 512], P(None, 'gz', 'gy', 'gx')
Inputs may be any that keep to these rules, and one draw needn't show every extreme that they name: `tissue_tensors`: the tensors are symmetric and positive definite: each off-diagonal component is at most 0.3 times the geometric mean of its two diagonal components. `electrodes`: all 128 voxel indices are distinct; voxel (z, y, x) has index (z * 32 + y) * 512 + x.
All inputs are finite; a program needn't handle non-finite values.
Results may differ from a plain program's by a relative error of at most 0.0003.
Values sent between devices are 32-bit elements; how exact they have to be, the bound alone decides.
A program may use at most 64 MiB of HBM per device.

v0:
```python
import jax
import jax.numpy as jnp
from jax import lax
from jax.experimental import pallas as pl
from jax.experimental.pallas import tpu as pltpu
from jax.sharding import PartitionSpec as P

MESH = pl.DeviceIdType.MESH
HIGH = lax.Precision.HIGHEST
DEPTH = 3


def nt_dot(a, b):
    return lax.dot_general(
        a, b, (((1,), (1,)), ((), ())), precision=HIGH, preferred_element_type=jnp.float32
    )


def nn_dot(a, b):
    return lax.dot_general(
        a, b, (((1,), (0,)), ((), ())), precision=HIGH, preferred_element_type=jnp.float32
    )


def make_krylov(nz, ny, nx, leads, rows, cols, classes):
    windowed = nz > DEPTH + 1
    layers = 2 * DEPTH + 1 if windowed else nz
    lead8 = leads + 8
    ext = rows + 2 * DEPTH
    top = DEPTH + rows
    if windowed:
        offsets = [d for d in range(-DEPTH, DEPTH + 1) if d]
    else:
        offsets = list(range(1, nz))
    noff = len(offsets)
    plane = nz * ny
    size = 2 * leads
    share = size // plane

    def kernel(
        table_hbm, labels_hbm, electrodes_hbm, field_hbm, base_out, gram_out,
        table, labels, electrodes, field, lsem,
        xe, re, qe, coef, inside, elec, xs, xr, gs, rs, zs,
        zsend, zrecv, ysend, yrecv, xsend, xrecv, asend, arecv,
    ):
        z, y, x = lax.axis_index("gz"), lax.axis_index("gy"), lax.axis_index("gx")
        me = z * ny + y
        own = DEPTH if windowed else z
        first = z - DEPTH if windowed else 0

        def plane_peer(k):
            peer = lax.rem(me + k, plane)
            return peer, {"gz": peer // ny, "gy": lax.rem(peer, ny)}

        loads = [
            pltpu.make_async_copy(source, target, lsem.at[i])
            for i, (source, target) in enumerate(
                (
                    (field_hbm, field), (labels_hbm, labels),
                    (electrodes_hbm, electrodes), (table_hbm, table),
                )
            )
        ]
        for load in loads:
            load.start()
        barrier = pltpu.get_barrier_semaphore()
        for k in range(1, plane):
            pl.semaphore_signal(
                barrier, inc=1, device_id=plane_peer(k)[1], device_id_type=MESH
            )
        for k in range(1, nx):
            pl.semaphore_signal(
                barrier, inc=1, device_id={"gx": lax.rem(x + k, nx)}, device_id_type=MESH
            )

        def fill(slot, lo, hi):
            for r in range(lo, hi):
                xe[slot, r, 0:leads, 0:cols] = jnp.zeros((leads, cols), jnp.float32)
                xe[slot, r, leads:lead8, 0:cols] = jnp.full((8, cols), -1.0, jnp.float32)

        if windowed:
            for s in range(layers):

                @pl.when((first + s < 0) | (first + s >= nz))
                def _(s=s):
                    fill(s, 0, ext)

        for s in range(layers):

            @pl.when(y == 0)
            def _(s=s):
                fill(s, 0, DEPTH)

            @pl.when(y == ny - 1)
            def _(s=s):
                fill(s, top, ext)

        for side, edge in ((0, nx - 1), (1, 0)):

            @pl.when(x == edge)
            def _(side=side):
                for s in range(layers):
                    xr[side, s, 0:leads] = jnp.zeros((leads, cols), jnp.float32)
                    xr[side, s, leads:lead8] = jnp.full((8, cols), -1.0, jnp.float32)

        for load in loads:
            load.wait()
        for r in range(rows):
            xe[own, DEPTH + r, 0:leads, 0:cols] = field[pl.ds(r, leads, stride=rows), :]
            xe[own, DEPTH + r, leads:lead8, 0:cols] = jnp.broadcast_to(
                labels[r : r + 1, :].astype(jnp.float32), (8, cols)
            )
        pl.semaphore_wait(barrier, plane - 1 + nx - 1)

        chunks = ((DEPTH, 2 * DEPTH), (top - DEPTH, top), (2 * DEPTH, top - DEPTH))

        def z_plan(i):
            d = offsets[i]
            if windowed:
                return (
                    z + d, DEPTH - d, DEPTH - d,
                    (z + d >= 0) & (z + d < nz), (z - d >= 0) & (z - d < nz),
                )
            return lax.rem(z + d, nz), z, lax.rem(z - d + nz, nz), None, None

        def when(cond, action):
            if cond is None:
                action()
            else:
                pl.when(cond)(action)

        def z_copy(i, c):
            peer, slot, _, _, _ = z_plan(i)
            lo, hi = chunks[c]
            return pltpu.make_async_remote_copy(
                src_ref=xe.at[own, lo:hi, :, 0:cols],
                dst_ref=xe.at[slot, lo:hi, :, 0:cols],
                send_sem=zsend.at[i, c],
                recv_sem=zrecv.at[i, c],
                device_id={"gz": peer},
                device_id_type=MESH,
            )

        def y_copy(i, slot, up):
            src = (top - DEPTH, top) if up else (DEPTH, 2 * DEPTH)
            dst = (0, DEPTH) if up else (top, ext)
            return pltpu.make_async_remote_copy(
                src_ref=xe.at[slot, src[0] : src[1], :, 0:cols],
                dst_ref=xe.at[slot, dst[0] : dst[1], :, 0:cols],
                send_sem=ysend.at[i, up],
                recv_sem=yrecv.at[i, up],
                device_id={"gy": y + 1 if up else y - 1},
                device_id_type=MESH,
            )

        has_low, has_high = y > 0, y < ny - 1

        def y_start(i, slot, up):
            pl.when(has_high if up else has_low)(lambda: y_copy(i, slot, up).start())

        def z_start(c):
            for i in range(noff):
                when(z_plan(i)[3], lambda i=i: z_copy(i, c).start())

        z_start(0)
        z_start(1)
        for up in (0, 1):
            y_start(noff, own, up)

        eye = lax.broadcasted_iota(jnp.int32, (leads, leads), 0) == lax.broadcasted_iota(
            jnp.int32, (leads, leads), 1
        )
        for e in range(2):
            line = electrodes[e : e + 1, :].astype(jnp.float32)
            column = jnp.sum(
                jnp.where(eye, jnp.broadcast_to(line, (leads, leads)), 0.0), axis=1, keepdims=True
            )
            elec[e] = jnp.broadcast_to(column, (leads, 2 * cols))

        def y_wait(i, slot, up):
            pl.when(has_high if up else has_low)(lambda: y_copy(i, slot, up).wait_send())
            pl.when(has_low if up else has_high)(lambda: y_copy(i, slot, up).wait_recv())

        def group(c):
            return pl.ds(pl.multiple_of(c * 8, 8), 8)

        lane = lax.broadcasted_iota(jnp.int32, (8, cols), 1)

        def pack(c, s):
            total = jnp.zeros((8, cols), jnp.float32)
            for r in range(ext):
                moved = pltpu.roll(xe[s, r, group(c), 0:cols], 8 * r, axis=1) if r else xe[
                    s, r, group(c), 0:cols
                ]
                shifted = lane + DEPTH if r == 0 else lane - (8 * r - DEPTH)
                keep = (shifted >= 0) & (shifted < 2 * DEPTH)
                if r == 0:
                    keep = (lane < DEPTH) | (lane >= cols - DEPTH)
                total = jnp.where(keep, moved, total)
            xs[s, group(c), :] = total
            return s

        def x_copy(side, i, slot):
            return pltpu.make_async_remote_copy(
                src_ref=xs.at[slot],
                dst_ref=xr.at[side, slot],
                send_sem=xsend.at[side, i],
                recv_sem=xrecv.at[side, i],
                device_id={"gx": x + 1 if side else x - 1},
                device_id_type=MESH,
            )

        sends = (x > 0, x < nx - 1)

        def x_start(i, slot):
            lax.fori_loop(0, lead8 // 8, pack, slot)
            for side in (0, 1):
                pl.when(sends[side])(lambda side=side: x_copy(side, i, slot).start())

        def x_wait(i, slot):
            for side in (0, 1):
                pl.when(sends[side])(lambda side=side: x_copy(side, i, slot).wait_send())
                pl.when(sends[1 - side])(lambda side=side: x_copy(side, i, slot).wait_recv())

        for up in (0, 1):
            y_wait(noff, own, up)
        x_start(noff, own)

        for c in range(2):
            for i in range(noff):

                def arrived(i=i, c=c):
                    z_copy(i, c).wait_recv()
                    y_start(i, z_plan(i)[2], c)

                when(z_plan(i)[4], arrived)
            if c == 0:
                z_start(2)
        for i in range(noff):
            when(z_plan(i)[4], lambda i=i: z_copy(i, 2).wait_recv())

        for up in (0, 1):
            for i in range(noff):
                when(z_plan(i)[4], lambda i=i, up=up: y_wait(i, z_plan(i)[2], up))
        for i in range(noff):
            x_start(i, z_plan(i)[2])
        for c in range(3):
            for i in range(noff):
                when(z_plan(i)[3], lambda i=i, c=c: z_copy(i, c).wait_send())
        x_wait(noff, own)
        for i in range(noff):
            x_wait(i, z_plan(i)[2])

        near = (lane & 7) < 4
        rim = (lane < DEPTH) | (lane >= cols - DEPTH)

        def unpack(c, _):
            outside = jnp.where(c == leads // 8, -1.0, 0.0)
            for s in range(layers):
                both = jnp.where(near, xr[0, s, group(c), :], xr[1, s, group(c), :])
                for r in range(ext):
                    moved = pltpu.roll(both, cols - 8 * r, axis=1) if r else both
                    xe[s, r, group(c), cols : 2 * cols] = jnp.where(rim, moved, outside)
            return 0

        lax.fori_loop(0, lead8 // 8, unpack, 0)

        values = [[table[i, t] for t in range(table.shape[1])] for i in range(6)]

        def lookup(r, _):
            for s in range(layers):
                label = xe[s, r, leads:lead8, :]
                parts = [jnp.zeros(label.shape, jnp.float32)] * 6
                for t in range(table.shape[1]):
                    match = label == float(t)
                    parts = [jnp.where(match, values[i][t], parts[i]) for i in range(6)]
                for i in range(6):
                    coef[i, s, r] = parts[i]
                inside[s, r] = jnp.where(label >= 0.0, 1.0, 0.0)
            return 0

        lax.fori_loop(0, ext, lookup, 0)

        wide = 2 * cols
        lanes = lax.broadcasted_iota(jnp.int32, (8, wide), 1)
        column_id = x * cols + jnp.where(lanes >= cols + cols // 2, lanes - wide, lanes)

        def operate(source, emit, lo, hi, c):
            below_y = [None] * layers
            for r in range(lo - 1, hi):
                here = [source[s, r, group(c), :] for s in range(layers)]
                below_z = None
                for s in range(layers):
                    t = [coef[i, s, r] for i in range(6)]
                    v = here[s]
                    grad_x = pltpu.roll(v, wide - 1, axis=1) - v
                    grad_y = source[s, r + 1, group(c), :] - v
                    grad_z = here[s + 1] - v if s + 1 < layers else -v
                    flux_y = t[3] * grad_x + t[1] * grad_y + t[5] * grad_z
                    if r >= lo:
                        flux_x = t[0] * grad_x + t[3] * grad_y + t[4] * grad_z
                        flux_z = t[4] * grad_x + t[5] * grad_y + t[2] * grad_z
                        total = (below_y[s] - flux_y) + (pltpu.roll(flux_x, 1, axis=1) - flux_x)
                        total = total - flux_z if below_z is None else total + (below_z - flux_z)
                        emit(s, r, c, total * inside[s, r])
                        below_z = flux_z
                    below_y[s] = flux_y

        def emit_r(s, r, c, value):
            row_id = (first + s) * (ny * rows) + y * rows + (r - DEPTH)
            voxel = (row_id * (nx * cols) + column_id).astype(jnp.float32)
            source = jnp.where(elec[0, group(c), :] == voxel, 1.0, 0.0) - jnp.where(
                elec[1, group(c), :] == voxel, 1.0, 0.0
            )
            re[s, r, group(c), :] = source * inside[s, r] - value

        def emit_q(s, r, c, value):
            qe[s, r, group(c), :] = value

        def emit_p(s, r, c, value):
            xe[s, r, group(c), 0:cols] = value[:, 0:cols]

        def loop(source, emit, lo, hi):
            def step(c, _):
                operate(source, emit, lo, hi, c)
                return 0

            lax.fori_loop(0, leads // 8, step, 0)

        loop(xe, emit_r, 1, ext - 1)
        loop(re, emit_q, 2, ext - 2)
        loop(qe, emit_p, 3, ext - 3)
        for r in range(rows):
            at = slice(r * cols, (r + 1) * cols)
            base_out[0:leads, at] = re[own, DEPTH + r, :, 0:cols]
            base_out[leads : 2 * leads, at] = qe[own, DEPTH + r, :, 0:cols]
            base_out[2 * leads : 3 * leads, at] = xe[own, DEPTH + r, 0:leads, 0:cols]
        upper = nt_dot(base_out[0:leads, :], base_out[0 : 2 * leads, :])
        lower = nt_dot(base_out[leads : 2 * leads, :], base_out[leads : 3 * leads, :])
        grams = jnp.concatenate([upper, lower], axis=0)
        for i in range(plane):
            gs[i] = grams[i * share : (i + 1) * share, :]

        def a_copy(phase, k, src, dst, device):
            return pltpu.make_async_remote_copy(
                src_ref=src, dst_ref=dst,
                send_sem=asend.at[phase, k], recv_sem=arecv.at[phase, k],
                device_id=device, device_id_type=MESH,
            )

        def scatter(k):
            peer, device = plane_peer(k)
            return a_copy(0, k, gs.at[peer], rs.at[me], device)

        def along(k):
            return a_copy(1, k, zs.at[x], zs.at[x], {"gx": lax.rem(x + k, nx)})

        def gather(k):
            return a_copy(2, k, gram_out.at[me], gram_out.at[me], plane_peer(k)[1])

        def exchange(copy, count):
            for k in range(1, count):
                copy(k).start()
            for k in range(1, count):
                copy(k).wait()

        rs[me] = gs[me]
        exchange(scatter, plane)
        zs[x] = jnp.sum(rs[...], axis=0)
        exchange(along, nx)
        gram_out[me] = jnp.sum(zs[...], axis=0)
        exchange(gather, plane)

    vmem = pl.BlockSpec(memory_space=pltpu.VMEM)
    f32 = jnp.float32
    group_sems = pltpu.SemaphoreType.DMA((3, max(plane, nx)))
    call = pl.pallas_call(
        kernel,
        out_shape=(
            jax.ShapeDtypeStruct((3 * leads, rows * cols), f32),
            jax.ShapeDtypeStruct((plane, share, size), f32),
        ),
        in_specs=[pl.BlockSpec(memory_space=pltpu.HBM)] * 4,
        out_specs=(vmem, vmem),
        scratch_shapes=[
            pltpu.SMEM((6, classes), f32),
            pltpu.VMEM((rows, cols), jnp.int32),
            pltpu.VMEM((2, leads), jnp.int32),
            pltpu.VMEM((leads * rows, cols), f32),
            pltpu.SemaphoreType.DMA((4,)),
            pltpu.VMEM((layers, ext, lead8, 2 * cols), f32),
            pltpu.VMEM((layers, ext, leads, 2 * cols), f32),
            pltpu.VMEM((layers, ext, leads, 2 * cols), f32),
            pltpu.VMEM((6, layers, ext, 8, 2 * cols), f32),
            pltpu.VMEM((layers, ext, 8, 2 * cols), f32),
            pltpu.VMEM((2, leads, 2 * cols), f32),
            pltpu.VMEM((layers, lead8, cols), f32),
            pltpu.VMEM((2, layers, lead8, cols), f32),
            pltpu.VMEM((plane, share, size), f32),
            pltpu.VMEM((plane, share, size), f32),
            pltpu.VMEM((nx, share, size), f32),
            pltpu.SemaphoreType.DMA((noff, 3)),
            pltpu.SemaphoreType.DMA((noff, 3)),
            pltpu.SemaphoreType.DMA((noff + 1, 2)),
            pltpu.SemaphoreType.DMA((noff + 1, 2)),
            pltpu.SemaphoreType.DMA((2, noff + 1)),
            pltpu.SemaphoreType.DMA((2, noff + 1)),
            group_sems,
            group_sems,
        ],
        compiler_params=pltpu.CompilerParams(
            collective_id=0, has_side_effects=True,
            vmem_limit_bytes=(8 + 7 * layers) * 1024 * 1024,
        ),
        name="krylov",
    )
    return call, size


def eliminate(matrix, count):
    row_id = lax.broadcasted_iota(jnp.int32, (8, 1), 0)
    matrix = matrix * (1.0 / matrix[0:1, 0:1])
    tiles = [matrix[i : i + 8, :] for i in range(0, count, 8)]
    for k in range(0, count, 2):
        home, row = divmod(k, 8)
        one, two = tiles[home][row : row + 1, :], tiles[home][row + 1 : row + 2, :]
        left = [jnp.broadcast_to(tile[:, k : k + 1], tile.shape) for tile in tiles]
        right = [jnp.broadcast_to(tile[:, k + 1 : k + 2], tile.shape) for tile in tiles]
        p11, p21 = left[home][row : row + 1, :], left[home][row + 1 : row + 2, :]
        p12, p22 = right[home][row : row + 1, :], right[home][row + 1 : row + 2, :]
        inverse = 1.0 / (p11 * p22 - p12 * p21)
        first = (p22 * inverse) * one - (p12 * inverse) * two
        second = (p11 * inverse) * two - (p21 * inverse) * one
        tiles = [
            tile - left[i] * first - right[i] * second for i, tile in enumerate(tiles)
        ]
        tiles[home] = jnp.where(
            row_id == row, first, jnp.where(row_id == row + 1, second, tiles[home])
        )
    return jnp.concatenate(tiles, axis=0)


def make_combine(leads, rows, cols):
    def kernel(gram, base, field, out, res):
        rr, rq = gram[0:leads, 0:leads], gram[0:leads, leads : 2 * leads]
        qq, qp = gram[leads : 2 * leads, 0:leads], gram[leads : 2 * leads, leads : 2 * leads]
        first = eliminate(jnp.concatenate([rq, rr, qq], axis=1), leads)
        z2, z1 = first[:, leads : 2 * leads], first[:, 2 * leads : 3 * leads]
        schur = jnp.concatenate([qp, rq], axis=1) - nn_dot(qq, jnp.concatenate([z1, z2], axis=1))
        e = eliminate(schur, leads)[:, leads : 2 * leads]
        c = z2 - nn_dot(z1, e)
        mix = jnp.transpose(jnp.concatenate([c, e], axis=0))
        gain = nn_dot(mix, base[0 : 2 * leads, :])
        loss = nn_dot(mix, base[leads : 3 * leads, :])
        for r in range(rows):
            at = slice(r * cols, (r + 1) * cols)
            spread = pl.ds(r, leads, stride=rows)
            out[spread, :] = field[spread, :] + gain[:, at]
            res[spread, :] = base[0:leads, at] - loss[:, at]

    vmem = pl.BlockSpec(memory_space=pltpu.VMEM)
    shape = jax.ShapeDtypeStruct((leads * rows, cols), jnp.float32)
    return pl.pallas_call(
        kernel,
        out_shape=(shape, shape),
        in_specs=[vmem] * 3,
        out_specs=(vmem, vmem),
        compiler_params=pltpu.CompilerParams(vmem_limit_bytes=24 * 1024 * 1024),
        name="combine",
    )


def solution(mesh):
    nz, ny, nx = (mesh.shape[name] for name in ("gz", "gy", "gx"))

    def body(labels, tissue_tensors, electrodes, initial):
        leads, _, rows, cols = initial.shape
        field = initial.reshape(leads * rows, cols)
        krylov, size = make_krylov(
            nz, ny, nx, leads, rows, cols, tissue_tensors.shape[1]
        )
        base, gram = krylov(tissue_tensors, labels.reshape(rows, cols), electrodes, field)
        out, res = make_combine(leads, rows, cols)(gram.reshape(size, size), base, field)
        return out.reshape(initial.shape), res.reshape(initial.shape)

    placed = (P("gz", "gy", "gx"), P(), P(), P(None, "gz", "gy", "gx"))
    return jax.shard_map(
        body,
        mesh=mesh,
        in_specs=placed,
        out_specs=(P(None, "gz", "gy", "gx"), P(None, "gz", "gy", "gx")),
        check_vma=False,
    )
```

profile of v0, /device:TPU:0, one launch (start us, length us, event | category | flops | bytes accessed | tf_op | source)
XLA Modules:
  0.0 49.0 jit_solution(2669460004839048469)
XLA Ops:
  0.6 0.0 copy-start.4
  0.6 0.7 %copy-done.4 = s32[2,64]{1,0:T(2,128)S(1)} copy-done((s32[2,64]{1,0:T(2,128)S(1)}, s32[2,64]{1,0:T(2,128)}, u32[]{:S(2)}) %copy-start.4) | copy-done | bytes 536
  1.3 0.0 copy-start
  1.3 0.9 %copy-done = f32[64,1,8,128]{3,2,1,0:T(8,128)S(1)} copy-done((f32[64,1,8,128]{3,2,1,0:T(8,128)S(1)}, f32[64,1,8,128]{3,2,1,0:T(8,128)}, u32[]{:S(2)}) %copy-start) | copy-done | bytes 262168
  2.3 0.0 copy-start.2
  2.3 0.7 %copy-done.2 = f32[6,8]{1,0:T(8,128)S(1)} copy-done((f32[6,8]{1,0:T(8,128)S(1)}, f32[6,8]{1,0:T(8,128)}, u32[]{:S(2)}) %copy-start.2) | copy-done | bytes 216
  2.9 0.0 copy-start.3
  3.0 0.7 %copy-done.3 = s32[1,8,128]{2,1,0:T(8,128)S(1)} copy-done((s32[1,8,128]{2,1,0:T(8,128)S(1)}, s32[1,8,128]{2,1,0:T(8,128)}, u32[]{:S(2)}) %copy-start.3) | copy-done | bytes 4120
  3.6 0.0 copy-start.1
  3.6 36.8 %krylov.1 = (f32[192,1024]{1,0:T(8,128)S(1)}, f32[8,16,128]{2,1,0:T(8,128)S(1)}) custom-call(f32[6,8]{1,0:T(8,128)S(1)} %copy-done.2, s32[8,128]{1,0:T(8,128)S(1)} %bitcast.12, s32[2,64]{1,0:T(2,128)S(1)} %copy-done.4, f32[512,128]{1,0:T(8,128)S(1)} %bitcast.9), custom_call_target="tpu_custom_call" | custom-call | tf_op jit(solution)/shard_map/krylov/pallas_call | solution.py:482
  40.4 0.0 copy-done.1
  40.4 8.6 %combine.1 = (f32[512,128]{1,0:T(8,128)}, f32[512,128]{1,0:T(8,128)}) custom-call(f32[128,128]{1,0:T(8,128)S(1)} %bitcast.11, f32[192,1024]{1,0:T(8,128)S(1)} %get-tuple-element.7.base, f32[512,128]{1,0:T(8,128)S(1)} %bitcast.10), custom_call_target="tpu_custom_call" | custom-call | tf_op jit(solution)/shard_map/combine/pallas_call | solution.py:483
Async XLA Ops:
  0.6 0.7 %copy-start.4 = (s32[2,64]{1,0:T(2,128)S(1)}, s32[2,64]{1,0:T(2,128)}, u32[]{:S(2)}) copy-start(s32[2,64]{1,0:T(2,128)} %electrodes_hbm.1) | copy-start | bytes 1540
  1.3 0.9 %copy-start = (f32[64,1,8,128]{3,2,1,0:T(8,128)S(1)}, f32[64,1,8,128]{3,2,1,0:T(8,128)}, u32[]{:S(2)}) copy-start(f32[64,1,8,128]{3,2,1,0:T(8,128)} %param.7) | copy-start | bytes 786436
  2.3 0.7 %copy-start.2 = (f32[6,8]{1,0:T(8,128)S(1)}, f32[6,8]{1,0:T(8,128)}, u32[]{:S(2)}) copy-start(f32[6,8]{1,0:T(8,128)} %table_hbm.1) | copy-start | bytes 580
  2.9 0.7 %copy-start.3 = (s32[1,8,128]{2,1,0:T(8,128)S(1)}, s32[1,8,128]{2,1,0:T(8,128)}, u32[]{:S(2)}) copy-start(s32[1,8,128]{2,1,0:T(8,128)} %param.4) | copy-start | bytes 12292
  3.6 36.8 %copy-start.1 = (f32[64,1,8,128]{3,2,1,0:T(8,128)S(1)}, f32[64,1,8,128]{3,2,1,0:T(8,128)}, u32[]{:S(2)}) copy-start(f32[64,1,8,128]{3,2,1,0:T(8,128)} %param.7) | copy-start | bytes 786436
where the time goes:
time: 49.3 us; the launch traced here: 49 us
  Pallas kernels  45.4 us (92%)
  local copies, waits for them, and re-layouts  3 us (6%)
  between operations  0.66 us (1%)
    pallas_call x1, Pallas kernels, body(): krylov(tissue_tensors, labels.reshape(rows, cols), electrodes, field)  36.8 us
    pallas_call x1, Pallas kernels, body(): make_combine(leads, rows, cols)(gram.reshape(size, size), base, field)  8.61 us
    unnamed x10, local copies, waits for them, and re-layouts  3 us

commit v1 on v0

v1 whole, which is shorter than its diff:
```python
import jax
import jax.numpy as jnp
from jax import lax
from jax.experimental import pallas as pl
from jax.experimental.pallas import tpu as pltpu
from jax.sharding import PartitionSpec as P

MESH = pl.DeviceIdType.MESH
HIGH = lax.Precision.HIGHEST
DEPTH = 3
VMEM_LIMIT = 58 * 1024 * 1024


def nt_dot(a, b):
    return lax.dot_general(
        a, b, (((1,), (1,)), ((), ())), precision=HIGH, preferred_element_type=jnp.float32
    )


def nn_dot(a, b):
    return lax.dot_general(
        a, b, (((1,), (0,)), ((), ())), precision=HIGH, preferred_element_type=jnp.float32
    )


def make_krylov(nz, ny, nx, leads, rows, cols, classes):
    windowed = nz > DEPTH + 1
    layers = 2 * DEPTH + 1 if windowed else nz
    ext = rows + 2 * DEPTH
    top = DEPTH + rows
    if windowed:
        offsets = [d for d in range(-DEPTH, DEPTH + 1) if d]
    else:
        offsets = list(range(1, nz))
    noff = len(offsets)
    groups = leads // 8
    per = 2
    nch = groups // per
    span = per * 8
    plane = nz * ny
    size = 2 * leads
    flat = plane * nx <= 64
    owners = plane * nx if flat else plane
    share = size // owners
    last = cols - 1

    def kernel(
        table_hbm, labels_hbm, electrodes_hbm, field_hbm, base_hbm, gram_hbm,
        base_out, total, ssem, table, labels, electrodes, field, lsem,
        xe, lt, lab, lp, lr, xs, xr, re, qe, pe, coef, inside, hcoef, hinside, elec, gs, rs, zs,
        zsend, zrecv, ysend, yrecv, xsend, xrecv, asend, arecv,
    ):
        z, y, x = lax.axis_index("gz"), lax.axis_index("gy"), lax.axis_index("gx")
        own = DEPTH if windowed else z
        first = z - DEPTH if windowed else 0
        zs_ = [lax.rem(z + d, nz) for d in range(nz)]
        ys_ = [lax.rem(y + d, ny) for d in range(ny)]
        xs_ = [lax.rem(x + d, nx) for d in range(nx)]
        plane_peers = [
            (zs_[dz] * ny + ys_[dy], {"gz": zs_[dz], "gy": ys_[dy]})
            for dz in range(nz)
            for dy in range(ny)
        ]
        line_peers = [(xs_[dx], {"gx": xs_[dx]}) for dx in range(nx)]
        if flat:
            all_peers = [
                (pid * nx + xid, {**pdev, **xdev})
                for pid, pdev in plane_peers
                for xid, xdev in line_peers
            ]
            greeted = all_peers[1:]
        else:
            greeted = plane_peers[1:] + line_peers[1:]

        loads = [
            pltpu.make_async_copy(source, target, lsem.at[i])
            for i, (source, target) in enumerate(
                (
                    (field_hbm, field), (labels_hbm, labels),
                    (electrodes_hbm, electrodes), (table_hbm, table),
                )
            )
        ]
        for load in loads:
            load.start()
        barrier = pltpu.get_barrier_semaphore()
        for _, device in greeted:
            pl.semaphore_signal(barrier, inc=1, device_id=device, device_id_type=MESH)

        outside = jnp.full((8, cols), -1.0, jnp.float32)

        def fill(slot, lo, hi):
            for r in range(lo, hi):
                xe[slot, r] = jnp.zeros((leads, cols), jnp.float32)

        if windowed:
            for s in range(layers):

                @pl.when((first + s < 0) | (first + s >= nz))
                def _(s=s):
                    fill(s, 0, ext)
                    for j in range(3):
                        lt[s, j] = outside

        for s in range(layers):

            @pl.when(y == 0)
            def _(s=s):
                fill(s, 0, DEPTH)
                lt[s, 1] = outside

            @pl.when(y == ny - 1)
            def _(s=s):
                fill(s, top, ext)
                lt[s, 2] = outside

        for side, edge in ((0, nx - 1), (1, 0)):

            @pl.when(x == edge)
            def _(side=side):
                for s in range(layers):
                    xr[side, s] = jnp.zeros((leads, cols), jnp.float32)
                    lr[side, s] = outside

        for load in loads:
            load.wait()
        lt[own, 0] = labels[...].astype(jnp.float32)
        for r in range(rows):
            xe[own, DEPTH + r] = field[pl.ds(r, leads, stride=rows), :]
        pl.semaphore_wait(barrier, len(greeted))

        def z_plan(i):
            d = offsets[i]
            if windowed:
                return (
                    z + d, DEPTH - d, DEPTH - d,
                    (z + d >= 0) & (z + d < nz), (z - d >= 0) & (z - d < nz),
                )
            return lax.rem(z + d, nz), z, lax.rem(z - d + nz, nz), None, None

        def when(cond, action):
            if cond is None:
                action()
            else:
                pl.when(cond)(action)

        def remote(src, dst, send, recv, device):
            return pltpu.make_async_remote_copy(
                src_ref=src, dst_ref=dst, send_sem=send, recv_sem=recv,
                device_id=device, device_id_type=MESH,
            )

        def chunk(c):
            if c is None:
                return slice(0, leads)
            if isinstance(c, int):
                return slice(c * span, (c + 1) * span)
            return pl.ds(pl.multiple_of(c * span, 8), span)

        def z_copies(i, c):
            peer, slot, _, _, _ = z_plan(i)
            device = {"gz": peer}
            body = remote(
                xe.at[own, DEPTH:top, chunk(c), :], xe.at[slot, DEPTH:top, chunk(c), :],
                zsend.at[i, c], zrecv.at[i, c], device,
            )
            if c != 0:
                return [body]
            return [
                remote(lt.at[own, 0], lt.at[slot, 0], zsend.at[i, nch], zrecv.at[i, nch], device),
                body,
            ]

        def y_copies(i, slot, up, c, tile):
            src = (top - DEPTH, top) if up else (DEPTH, 2 * DEPTH)
            dst = (0, DEPTH) if up else (top, ext)
            device = {"gy": y + 1 if up else y - 1}
            at = 0 if c is None else c
            copies = [
                remote(
                    xe.at[slot, src[0] : src[1], chunk(c), :],
                    xe.at[slot, dst[0] : dst[1], chunk(c), :],
                    ysend.at[i, up, at], yrecv.at[i, up, at], device,
                )
            ]
            if tile:
                copies.insert(
                    0,
                    remote(
                        lt.at[slot, 0], lt.at[slot, 1 if up else 2],
                        ysend.at[i, up, nch], yrecv.at[i, up, nch], device,
                    ),
                )
            return copies

        def x_copies(i, slot, side, c, tile):
            device = {"gx": x + 1 if side else x - 1}
            at = 0 if c is None else c
            copies = [
                remote(
                    xs.at[slot, chunk(c), :], xr.at[side, slot, chunk(c), :],
                    xsend.at[i, side, at], xrecv.at[i, side, at], device,
                )
            ]
            if tile:
                copies.insert(
                    0,
                    remote(
                        lp.at[slot], lr.at[side, slot],
                        xsend.at[i, side, nch], xrecv.at[i, side, nch], device,
                    ),
                )
            return copies

        has_low, has_high = y > 0, y < ny - 1
        ysends = (has_low, has_high)
        xsends = (x > 0, x < nx - 1)

        def start(copies):
            for copy in copies:
                copy.start()

        def wait_send(copies):
            for copy in copies:
                copy.wait_send()

        def wait_recv(copies):
            for copy in copies:
                copy.wait_recv()

        def both(sends, make, action, mirrored=False):
            for side in (1, 0):
                pl.when(sends[1 - side if mirrored else side])(
                    lambda side=side: action(make(side))
                )

        for c in range(nch):
            for i in range(noff):
                when(z_plan(i)[3], lambda i=i, c=c: start(z_copies(i, c)))
            if c == 0:
                both(ysends, lambda up: y_copies(noff, own, up, None, True), start)

        eye = lax.broadcasted_iota(jnp.int32, (leads, leads), 0) == lax.broadcasted_iota(
            jnp.int32, (leads, leads), 1
        )
        for e in range(2):
            line = electrodes[e : e + 1, :].astype(jnp.float32)
            column = jnp.sum(
                jnp.where(eye, jnp.broadcast_to(line, (leads, leads)), 0.0), axis=1, keepdims=True
            )
            elec[e] = jnp.broadcast_to(column, (leads, cols))

        def group(c):
            return pl.ds(pl.multiple_of(c * 8, 8), 8)

        lane = lax.broadcasted_iota(jnp.int32, (8, cols), 1)

        def gather_edges(load):
            total = jnp.zeros((8, cols), jnp.float32)
            for r in range(ext):
                moved = pltpu.roll(load(r), 8 * r, axis=1) if r else load(r)
                if r == 0:
                    keep = (lane < DEPTH) | (lane >= cols - DEPTH)
                else:
                    keep = (lane >= 8 * r - DEPTH) & (lane < 8 * r + DEPTH)
                total = jnp.where(keep, moved, total)
            return total

        def pack(slot, lo, hi):
            def step(c, _):
                xs[slot, group(c), :] = gather_edges(lambda r: xe[slot, r, group(c), :])
                return 0

            lax.fori_loop(lo, hi, step, 0)

        def pack_labels(slot):
            for r in range(ext):
                if r < DEPTH:
                    row = lt[slot, 1, rows - DEPTH + r : rows - DEPTH + r + 1, :]
                elif r < top:
                    row = lt[slot, 0, r - DEPTH : r - DEPTH + 1, :]
                else:
                    row = lt[slot, 2, r - top : r - top + 1, :]
                lab[slot, r] = jnp.broadcast_to(row, (8, cols))
            lp[slot] = gather_edges(lambda r: lab[slot, r])

        def forward_y(c):
            for i in range(noff):

                def arrived(i=i):
                    wait_recv(z_copies(i, c))
                    slot = z_plan(i)[2]
                    both(ysends, lambda up: y_copies(i, slot, up, c, c == 0), start)

                when(z_plan(i)[4], arrived)

        def forward_x(c):
            tile = isinstance(c, int) and c == 0
            for i in range(noff):
                slot = z_plan(i)[2]

                def arrived(i=i, slot=slot):
                    make = lambda up: y_copies(i, slot, up, c, tile)
                    both(ysends, make, wait_recv, mirrored=True)

                when(z_plan(i)[4], arrived)
                if tile:
                    pack_labels(slot)
                pack(slot, c * per, (c + 1) * per)
                both(xsends, lambda side: x_copies(i, slot, side, c, tile), start)

        both(ysends, lambda up: y_copies(noff, own, up, None, True), wait_recv, mirrored=True)
        pack_labels(own)
        pack(own, 0, groups)
        both(xsends, lambda side: x_copies(noff, own, side, None, True), start)

        forward_y(0)
        for c in range(1, nch):
            forward_y(c)
            if c <= nch - 2:
                forward_x(c - 1)

        both(xsends, lambda side: x_copies(noff, own, side, None, True), wait_recv, mirrored=True)
        for i in range(noff):
            slot = z_plan(i)[2]
            both(
                xsends, lambda side: x_copies(i, slot, side, 0, True)[:1], wait_recv, mirrored=True
            )

        values = [[table[i, t] for t in range(table.shape[1])] for i in range(6)]

        def look(label):
            parts = [jnp.zeros(label.shape, jnp.float32)] * 6
            for t in range(table.shape[1]):
                match = label == float(t)
                parts = [jnp.where(match, values[i][t], parts[i]) for i in range(6)]
            return parts, jnp.where(label >= 0.0, 1.0, 0.0)

        near = (lane & 7) < 4

        def lookup(r, _):
            for s in range(layers):
                parts, here = look(lab[s, r])
                for i in range(6):
                    coef[i, s, r] = parts[i]
                inside[s, r] = here
            return 0

        lax.fori_loop(0, ext, lookup, 0)
        for s in range(layers):
            for side in (0, 1):
                label = (
                    jnp.where(near, lp[s], lr[1, s]) if side else jnp.where(near, lr[0, s], lp[s])
                )
                parts, here = look(label)
                for i in range(6):
                    hcoef[i, s, side] = parts[i]
                hinside[s, side] = here

        line_width = nx * cols
        column = (x * cols + lane).astype(jnp.float32)
        moved = jnp.where(lane >= cols - DEPTH, lane + DEPTH - cols, lane + DEPTH)
        packed_row = moved // 8
        packed_voxel = packed_row * line_width + (moved - packed_row * 8) + (
            x * cols + (y * rows - DEPTH) * line_width - DEPTH
        )
        ends = (lane == 0, lane == last)
        seam = (lane & 7) == 7

        def source(c, voxel):
            return jnp.where(
                elec[0, group(c), :] == voxel, 1.0,
                jnp.where(elec[1, group(c), :] == voxel, -1.0, 0.0),
            )

        def flux(t, axis, grads):
            order = ((0, 3, 4), (3, 1, 5), (4, 5, 2))[axis]
            return t[order[0]] * grads[0] + t[order[1]] * grads[1] + t[order[2]] * grads[2]

        def rim(fields, side, full):
            sums, edges = [], []
            below = None
            for s in range(layers):
                t = [hcoef[i, s, side] for i in range(6)]
                v = fields[s]
                grads = (
                    pltpu.roll(v, last, axis=1) - v,
                    pltpu.roll(v, cols - 8, axis=1) - v,
                    fields[s + 1] - v if s + 1 < layers else -v,
                )
                flux_x = flux(t, 0, grads)
                edges.append(flux_x)
                if full:
                    flux_y, flux_z = flux(t, 1, grads), flux(t, 2, grads)
                    total = (pltpu.roll(flux_y, 8, axis=1) - flux_y) + (
                        pltpu.roll(flux_x, 1, axis=1) - flux_x
                    )
                    total = total - flux_z if below is None else total + (below - flux_z)
                    below = flux_z
                    sums.append(total)
            return sums, edges

        def seams(right, edges):
            return [
                jnp.where(seam, edges[s], pltpu.roll(right[s], cols - 2, axis=1))
                for s in range(layers)
            ]

        def operate(load, emit, lo, hi, joins):
            below_y = [None] * layers
            for r in range(lo - 1, hi):
                here = [load(s, r) for s in range(layers)]
                below_z = None
                for s in range(layers):
                    t = [coef[i, s, r] for i in range(6)]
                    v = here[s]
                    join = pltpu.roll(joins[s], (cols + 1 - 8 * r) % cols, axis=1)
                    grads = (
                        jnp.where(ends[1], join, pltpu.roll(v, last, axis=1)) - v,
                        load(s, r + 1) - v,
                        here[s + 1] - v if s + 1 < layers else -v,
                    )
                    flux_y = flux(t, 1, grads)
                    if r >= lo:
                        flux_x, flux_z = flux(t, 0, grads), flux(t, 2, grads)
                        before = jnp.where(ends[0], join, pltpu.roll(flux_x, 1, axis=1))
                        total = (below_y[s] - flux_y) + (before - flux_x)
                        total = total - flux_z if below_z is None else total + (below_z - flux_z)
                        emit(s, r, total)
                        below_z = flux_z
                    below_y[s] = flux_y

        def advance(c):
            mine = [xs[s, group(c), :] for s in range(layers)]
            right = [jnp.where(near, xr[0, s, group(c), :], mine[s]) for s in range(layers)]
            left = [jnp.where(near, mine[s], xr[1, s, group(c), :]) for s in range(layers)]
            right_sum, _ = rim(right, 0, True)
            left_sum, left_edge = rim(left, 1, True)
            joins_v = seams(right, left_edge)
            plane_voxels = ny * rows * line_width

            def rim_r(total, s, side):
                voxel = packed_voxel + ((first + s) * plane_voxels + (0 if side else cols))
                return (source(c, voxel.astype(jnp.float32)) - total) * hinside[s, side]

            right_r = [rim_r(right_sum[s], s, 0) for s in range(layers)]
            left_r = [rim_r(left_sum[s], s, 1) for s in range(layers)]
            right_sum, _ = rim(right_r, 0, True)
            left_sum, left_edge = rim(left_r, 1, True)
            joins_r = seams(right_r, left_edge)
            right_q = [right_sum[s] * hinside[s, 0] for s in range(layers)]
            left_q = [left_sum[s] * hinside[s, 1] for s in range(layers)]
            _, left_edge = rim(left_q, 1, False)
            joins_q = seams(right_q, left_edge)

            def emit_r(s, r, total):
                row = (first + s) * (ny * rows) + y * rows + (r - DEPTH)
                voxel = column + (row * line_width).astype(jnp.float32)
                re[s, r] = (source(c, voxel) - total) * inside[s, r]

            def emit_q(s, r, total):
                qe[s, r] = total * inside[s, r]

            def emit_p(s, r, total):
                pe[s, r - DEPTH] = total

            operate(lambda s, r: xe[s, r, group(c), :], emit_r, 1, ext - 1, joins_v)
            operate(lambda s, r: re[s, r], emit_q, 2, ext - 2, joins_r)
            operate(lambda s, r: qe[s, r], emit_p, 3, ext - 3, joins_q)
            for r in range(rows):
                at = slice(r * cols, (r + 1) * cols)
                base_out[group(c), at] = re[own, DEPTH + r]
                base_out[group(c + groups), at] = qe[own, DEPTH + r]
                base_out[group(c + 2 * groups), at] = pe[own, r]

        def turn(c, _):
            @pl.when(c < 2)
            def _():
                forward_x(c + (nch - 2))

            for i in range(noff):
                slot = z_plan(i)[2]
                both(
                    xsends, lambda side: x_copies(i, slot, side, c, False), wait_recv,
                    mirrored=True,
                )

            def step(g, _):
                advance(c * per + g)
                return 0

            lax.fori_loop(0, per, step, 0)
            return 0

        lax.fori_loop(0, nch, turn, 0)

        upper = nt_dot(base_out[0:leads, :], base_out[0 : 2 * leads, :])
        lower = nt_dot(base_out[leads : 2 * leads, :], base_out[leads : 3 * leads, :])
        grams = jnp.concatenate([upper, lower], axis=0)
        for i in range(owners):
            gs[i] = grams[i * share : (i + 1) * share, :]

        save = pltpu.make_async_copy(base_out, base_hbm, ssem.at[0])
        save.start()

        def exchange(phase, peers, source_of, target):
            copies = [
                remote(source_of(pid), target, asend.at[phase, k], arecv.at[phase, k], device)
                for k, (pid, device) in enumerate(peers)
                if k
            ]
            start(copies)
            for copy in copies:
                copy.wait()

        peers = all_peers if flat else plane_peers
        me = peers[0][0]
        rs[me] = gs[me]
        exchange(0, peers, lambda pid: gs.at[pid], rs.at[me])
        if flat:
            total[...] = jnp.sum(rs[...], axis=0)
        else:
            zs[x] = jnp.sum(rs[...], axis=0)
            exchange(1, line_peers, lambda pid: zs.at[x], zs.at[x])
            total[...] = jnp.sum(zs[...], axis=0)
        keep = pltpu.make_async_copy(total, gram_hbm.at[me], ssem.at[1])
        keep.start()
        exchange(2, peers, lambda pid: total, gram_hbm.at[me])
        keep.wait()
        save.wait()

        both(ysends, lambda up: y_copies(noff, own, up, None, True), wait_send)
        both(xsends, lambda side: x_copies(noff, own, side, None, True), wait_send)
        for i in range(noff):
            slot = z_plan(i)[2]
            for c in range(nch):
                when(z_plan(i)[3], lambda i=i, c=c: wait_send(z_copies(i, c)))

                def sent(i=i, slot=slot, c=c):
                    both(ysends, lambda up: y_copies(i, slot, up, c, c == 0), wait_send)

                when(z_plan(i)[4], sent)
                both(xsends, lambda side: x_copies(i, slot, side, c, c == 0), wait_send)

    f32 = jnp.float32
    tile = (8, cols)
    group_sems = pltpu.SemaphoreType.DMA((3, max(owners, nx)))
    y_sems = pltpu.SemaphoreType.DMA((noff + 1, 2, nch + 1))
    z_sems = pltpu.SemaphoreType.DMA((noff, nch + 1))
    call = pl.pallas_call(
        kernel,
        out_shape=(
            jax.ShapeDtypeStruct((3 * leads, rows * cols), f32),
            jax.ShapeDtypeStruct((owners, share, size), f32),
        ),
        in_specs=[pl.BlockSpec(memory_space=pltpu.HBM)] * 4,
        out_specs=[pl.BlockSpec(memory_space=pltpu.HBM)] * 2,
        scratch_shapes=[
            pltpu.VMEM((3 * leads, rows * cols), f32),
            pltpu.VMEM((share, size), f32),
            pltpu.SemaphoreType.DMA((2,)),
            pltpu.SMEM((6, classes), f32),
            pltpu.VMEM((rows, cols), jnp.int32),
            pltpu.VMEM((2, leads), jnp.int32),
            pltpu.VMEM((leads * rows, cols), f32),
            pltpu.SemaphoreType.DMA((4,)),
            pltpu.VMEM((layers, ext, leads, cols), f32),
            pltpu.VMEM((layers, 3) + tile, f32),
            pltpu.VMEM((layers, ext) + tile, f32),
            pltpu.VMEM((layers,) + tile, f32),
            pltpu.VMEM((2, layers) + tile, f32),
            pltpu.VMEM((layers, leads, cols), f32),
            pltpu.VMEM((2, layers, leads, cols), f32),
            pltpu.VMEM((layers, ext) + tile, f32),
            pltpu.VMEM((layers, ext) + tile, f32),
            pltpu.VMEM((layers, rows) + tile, f32),
            pltpu.VMEM((6, layers, ext) + tile, f32),
            pltpu.VMEM((layers, ext) + tile, f32),
            pltpu.VMEM((6, layers, 2) + tile, f32),
            pltpu.VMEM((layers, 2) + tile, f32),
            pltpu.VMEM((2, leads, cols), f32),
            pltpu.VMEM((owners, share, size), f32),
            pltpu.VMEM((owners, share, size), f32),
            pltpu.VMEM((nx, share, size), f32),
            z_sems, z_sems, y_sems, y_sems, y_sems, y_sems, group_sems, group_sems,
        ],
        compiler_params=pltpu.CompilerParams(
            collective_id=0, has_side_effects=True,
            vmem_limit_bytes=VMEM_LIMIT,
        ),
        name="krylov",
    )
    return call, size


def spread_row(value, row):
    return jnp.broadcast_to(value[row : row + 1, :], (8, value.shape[1]))


def solve_four(columns, row, values, sub):
    p = [[spread_row(columns[j], row + i) for j in range(4)] for i in range(4)]
    det = p[0][0] * p[1][1] - p[0][1] * p[1][0]
    e = [
        [p[1][1] * p[0][j] - p[0][1] * p[1][j] for j in (2, 3)],
        [p[0][0] * p[1][j] - p[1][0] * p[0][j] for j in (2, 3)],
    ]
    m = [
        [det * p[i][j + 2] - (p[i][0] * e[0][j] + p[i][1] * e[1][j]) for j in range(2)]
        for i in (2, 3)
    ]
    first = 1.0 / det
    second = det / (m[0][0] * m[1][1] - m[0][1] * m[1][0])
    done = []
    for value in values:
        cut = lambda v: v[:, : value.shape[1]]
        u = [spread_row(value, row + j) for j in range(4)]
        ua = (cut(p[1][1]) * u[0] - cut(p[0][1]) * u[1]) * cut(first)
        ub = (cut(p[0][0]) * u[1] - cut(p[1][0]) * u[0]) * cut(first)
        t = [u[i] - (cut(p[i][0]) * ua + cut(p[i][1]) * ub) for i in (2, 3)]
        x2 = (cut(m[1][1]) * t[0] - cut(m[0][1]) * t[1]) * cut(second)
        x3 = (cut(m[0][0]) * t[1] - cut(m[1][0]) * t[0]) * cut(second)
        x0 = ua - (cut(e[0][0]) * x2 + cut(e[0][1]) * x3) * cut(first)
        x1 = ub - (cut(e[1][0]) * x2 + cut(e[1][1]) * x3) * cut(first)
        x = (x0, x1, x2, x3)
        value = value - (
            (cut(columns[0]) * x0 + cut(columns[1]) * x1)
            + (cut(columns[2]) * x2 + cut(columns[3]) * x3)
        )
        for j in range(4):
            value = jnp.where(cut(sub) == row + j, x[j], value)
        done.append(value)
    return done


def columns_of(tile, at):
    return [jnp.broadcast_to(tile[0][:, at + j : at + j + 1], (8, 128)) for j in range(8)]


def eliminate(matrix, count):
    width = matrix.shape[1]
    cuts = [(a, min(a + 128, width)) for a in range(0, width, 128)]
    lane = lax.broadcasted_iota(jnp.int32, (8, 128), 1)
    sub = lax.broadcasted_iota(jnp.int32, (8, 128), 0)
    tiles = []
    for i in range(0, count, 8):
        parts = [matrix[i : i + 8, a:b] for a, b in cuts]
        pivot = jnp.sum(jnp.where(lane == sub + i, parts[0], 0.0), axis=1, keepdims=True)
        inverse = 1.0 / jnp.broadcast_to(pivot, (8, 128))
        tiles.append([part * inverse[:, : part.shape[1]] for part in parts])
    for home in range(count // 8):
        soon = [home + 1] if home + 1 < len(tiles) else []
        left = {i: columns_of(tiles[i], home * 8) for i in soon}
        mine = columns_of(tiles[home], home * 8)
        parts = solve_four(mine[:4], 0, mine[4:] + tiles[home], sub)
        parts = solve_four(parts[:4], 4, parts[4:], sub)
        for i in soon:
            for h, (a, b) in enumerate(cuts):
                terms = [left[i][j][:, : b - a] * spread_row(parts[h], j) for j in range(8)]
                while len(terms) > 1:
                    terms = [terms[j] + terms[j + 1] for j in range(0, len(terms), 2)]
                tiles[i][h] = tiles[i][h] - terms[0]
        rest = [i for i in range(len(tiles)) if i != home and i not in soon]
        active = jnp.concatenate([tiles[i][0][:, :count] for i in rest], axis=0)
        solved = jnp.concatenate(parts, axis=1)
        blank = lambda n: [jnp.zeros((n, width), jnp.float32)] if n else []
        padded = jnp.concatenate(
            blank(home * 8) + [solved] + blank(count - 8 - home * 8), axis=0
        )
        change = nn_dot(active, padded)
        for n, i in enumerate(rest):
            for h, (a, b) in enumerate(cuts):
                tiles[i][h] = tiles[i][h] - change[n * 8 : n * 8 + 8, a:b]
        tiles[home] = parts
    return jnp.concatenate([jnp.concatenate(tile, axis=1) for tile in tiles], axis=0)


def make_combine(leads, rows, cols):
    def kernel(
        gram_hbm, base_hbm, field_hbm, out_hbm, res_hbm, gram, base, field, out, res, isem, osem
    ):
        loads = [
            pltpu.make_async_copy(source, target, isem.at[i])
            for i, (source, target) in enumerate(
                ((gram_hbm, gram), (base_hbm, base), (field_hbm, field))
            )
        ]
        for load in loads:
            load.start()
        loads[0].wait()
        rr, rq = gram[0:leads, 0:leads], gram[0:leads, leads : 2 * leads]
        qq, qp = gram[leads : 2 * leads, 0:leads], gram[leads : 2 * leads, leads : 2 * leads]
        first = eliminate(jnp.concatenate([rq, rr, qq], axis=1), leads)
        z2, z1 = first[:, leads : 2 * leads], first[:, 2 * leads : 3 * leads]
        schur = jnp.concatenate([qp, rq], axis=1) - nn_dot(qq, jnp.concatenate([z1, z2], axis=1))
        e = eliminate(schur, leads)[:, leads : 2 * leads]
        c = z2 - nn_dot(z1, e)
        mix = jnp.transpose(jnp.concatenate([c, e], axis=0))
        for load in loads[1:]:
            load.wait()
        gain = nn_dot(mix, base[0 : 2 * leads, :])
        for r in range(rows):
            at = slice(r * cols, (r + 1) * cols)
            spread = pl.ds(r, leads, stride=rows)
            out[spread, :] = field[spread, :] + gain[:, at]
        saves = [
            pltpu.make_async_copy(source, target, osem.at[i])
            for i, (source, target) in enumerate(((out, out_hbm), (res, res_hbm)))
        ]
        saves[0].start()
        loss = nn_dot(mix, base[leads : 3 * leads, :])
        for r in range(rows):
            at = slice(r * cols, (r + 1) * cols)
            res[pl.ds(r, leads, stride=rows), :] = base[0:leads, at] - loss[:, at]
        saves[1].start()
        for save in saves:
            save.wait()

    f32 = jnp.float32
    hbm = pl.BlockSpec(memory_space=pltpu.HBM)
    shape = jax.ShapeDtypeStruct((leads * rows, cols), f32)
    block = pltpu.VMEM((leads * rows, cols), f32)
    return pl.pallas_call(
        kernel,
        out_shape=(shape, shape),
        in_specs=[hbm] * 3,
        out_specs=(hbm, hbm),
        scratch_shapes=[
            pltpu.VMEM((2 * leads, 2 * leads), f32),
            pltpu.VMEM((3 * leads, rows * cols), f32),
            block, block, block,
            pltpu.SemaphoreType.DMA((3,)),
            pltpu.SemaphoreType.DMA((2,)),
        ],
        compiler_params=pltpu.CompilerParams(vmem_limit_bytes=VMEM_LIMIT),
        name="combine",
    )


def solution(mesh):
    nz, ny, nx = (mesh.shape[name] for name in ("gz", "gy", "gx"))

    def body(labels, tissue_tensors, electrodes, initial):
        leads, _, rows, cols = initial.shape
        field = initial.reshape(leads * rows, cols)
        krylov, size = make_krylov(
            nz, ny, nx, leads, rows, cols, tissue_tensors.shape[1]
        )
        base, gram = krylov(tissue_tensors, labels.reshape(rows, cols), electrodes, field)
        out, res = make_combine(leads, rows, cols)(gram.reshape(size, size), base, field)
        return out.reshape(initial.shape), res.reshape(initial.shape)

    placed = (P("gz", "gy", "gx"), P(), P(), P(None, "gz", "gy", "gx"))
    return jax.shard_map(
        body,
        mesh=mesh,
        in_specs=placed,
        out_specs=(P(None, "gz", "gy", "gx"), P(None, "gz", "gy", "gx")),
        check_vma=False,
    )
```

time: 49.3 us -> 43.3 us (0.88)
  local copies, waits for them, and re-layouts: 3 us -> 0 us
  Pallas kernels: 45.4 us -> 42.5 us
    unnamed x10 -> x0, local copies, waits for them, and re-layouts: 3 us -> none
    pallas_call x1, Pallas kernels: 36.8 us -> 35.2 us  [body(): krylov(tissue_tensors, labels.reshape(rows, cols), electrodes, field)]
    pallas_call x1, Pallas kernels: 8.61 us -> 7.32 us  [body(): make_combine(leads, rows, cols)(gram.reshape(size, size), base, field)]
where the time goes in v1:
time: 43.3 us; the launch traced here: 43.1 us
  Pallas kernels  42.5 us (98%)
  between operations  0.64 us (1%)
    pallas_call x1, Pallas kernels, body(): krylov(tissue_tensors, labels.reshape(rows, cols), electrodes, field)  35.2 us
    pallas_call x1, Pallas kernels, body(): make_combine(leads, rows, cols)(gram.reshape(size, size), base, field)  7.32 us

profile of v1, /device:TPU:0, one launch (start us, length us, event | category | flops | bytes accessed | tf_op | source)
XLA Modules:
  0.0 43.1 jit_solution(12823870487593504098)
XLA Ops:
  0.6 35.2 %krylov.1 = (f32[192,1024]{1,0:T(8,128)}, f32[32,4,128]{2,1,0:T(4,128)}) custom-call(f32[6,8]{1,0:T(8,128)} %table_hbm.1, s32[8,128]{1,0:T(8,128)} %bitcast.12, s32[2,64]{1,0:T(2,128)} %electrodes_hbm.1, f32[512,128]{1,0:T(8,128)} %bitcast.9), custom_call_target="tpu_custom_call" | custom-call | tf_op jit(solution)/shard_map/krylov/pallas_call | solution.py:748
  35.8 7.3 %combine.1 = (f32[512,128]{1,0:T(8,128)}, f32[512,128]{1,0:T(8,128)}) custom-call(f32[128,128]{1,0:T(8,128)} %bitcast.11, f32[192,1024]{1,0:T(8,128)} %get-tuple-element.7.base_hbm, f32[512,128]{1,0:T(8,128)} %bitcast.10), custom_call_target="tpu_custom_call" | custom-call | tf_op jit(solution)/shard_map/combine/pallas_call | solution.py:749

commit v2 on v1

--- a/solution.py
+++ b/solution.py
@@ -8,6 +8,9 @@
 MESH = pl.DeviceIdType.MESH
 HIGH = lax.Precision.HIGHEST
 DEPTH = 3
+CHUNKS = 2
+PAIR = 1
+TWIN = 4
 VMEM_LIMIT = 58 * 1024 * 1024
 
 
@@ -34,20 +37,19 @@
         offsets = list(range(1, nz))
     noff = len(offsets)
     groups = leads // 8
-    per = 2
+    per = groups // CHUNKS
     nch = groups // per
     span = per * 8
     plane = nz * ny
     size = 2 * leads
-    flat = plane * nx <= 64
-    owners = plane * nx if flat else plane
-    share = size // owners
+    share = size // plane
     last = cols - 1
+    lead8 = leads + 8
 
     def kernel(
         table_hbm, labels_hbm, electrodes_hbm, field_hbm, base_hbm, gram_hbm,
         base_out, total, ssem, table, labels, electrodes, field, lsem,
-        xe, lt, lab, lp, lr, xs, xr, re, qe, pe, coef, inside, hcoef, hinside, elec, gs, rs, zs,
+        xe, lt, lab, xs, xr, xm, joined, re, qe, pe, coef, inside, hcoef, hinside, elec, gs, rs, zs,
         zsend, zrecv, ysend, yrecv, xsend, xrecv, asend, arecv,
     ):
         z, y, x = lax.axis_index("gz"), lax.axis_index("gy"), lax.axis_index("gx")
@@ -62,15 +64,10 @@
             for dy in range(ny)
         ]
         line_peers = [(xs_[dx], {"gx": xs_[dx]}) for dx in range(nx)]
-        if flat:
-            all_peers = [
-                (pid * nx + xid, {**pdev, **xdev})
-                for pid, pdev in plane_peers
-                for xid, xdev in line_peers
-            ]
-            greeted = all_peers[1:]
-        else:
-            greeted = plane_peers[1:] + line_peers[1:]
+        corner_peers = [
+            (None, {"gy": ys_[dy], "gx": xs_[dx]}) for dy in (1, ny - 1) for dx in (1, nx - 1)
+        ]
+        greeted = plane_peers[1:] + line_peers[1:] + corner_peers
 
         loads = [
             pltpu.make_async_copy(source, target, lsem.at[i])
@@ -101,6 +98,8 @@
                     fill(s, 0, ext)
                     for j in range(3):
                         lt[s, j] = outside
+                    xm[s, 0:leads] = jnp.zeros((leads, cols), jnp.float32)
+                    xm[s, leads:lead8] = outside
 
         for s in range(layers):
 
@@ -114,19 +113,44 @@
                 fill(s, top, ext)
                 lt[s, 2] = outside
 
-        for side, edge in ((0, nx - 1), (1, 0)):
-
-            @pl.when(x == edge)
-            def _(side=side):
-                for s in range(layers):
-                    xr[side, s] = jnp.zeros((leads, cols), jnp.float32)
-                    lr[side, s] = outside
+        arrivals = (x < nx - 1, x > 0)
+        beside = (y > 0, None, y < ny - 1)
+
+        def exists(side, j):
+            return arrivals[side] if j == 1 else arrivals[side] & beside[j]
+
+        for side in (0, 1):
+            for j in range(3):
+
+                @pl.when(jnp.logical_not(exists(side, j)))
+                def _(side=side, j=j):
+                    xr[side, j, 0:leads] = jnp.zeros((leads, cols), jnp.float32)
+                    xr[side, j, leads:lead8] = outside
+
+        lane = lax.broadcasted_iota(jnp.int32, (8, cols), 1)
+
+        def group(c):
+            return pl.ds(pl.multiple_of(c * 8, 8), 8)
+
+        def gather_edges(load, lo, hi):
+            total = None
+            for r in reversed(range(lo, hi)):
+                moved = pltpu.roll(load(r), 8 * r, axis=1) if r else load(r)
+                if total is None:
+                    total = moved
+                    continue
+                keep = lane < 8 * r + DEPTH + 1
+                if r == 0:
+                    keep = keep | (lane >= cols - DEPTH)
+                total = jnp.where(keep, moved, total)
+            return total
 
         for load in loads:
             load.wait()
         lt[own, 0] = labels[...].astype(jnp.float32)
         for r in range(rows):
             xe[own, DEPTH + r] = field[pl.ds(r, leads, stride=rows), :]
+
         pl.semaphore_wait(barrier, len(greeted))
 
         def z_plan(i):
@@ -157,88 +181,97 @@
                 return slice(c * span, (c + 1) * span)
             return pl.ds(pl.multiple_of(c * span, 8), span)
 
-        def z_copies(i, c):
+        pieces = ((DEPTH, 2 * DEPTH), (top - DEPTH, top), (2 * DEPTH, top - DEPTH))
+
+        def z_copy(i, part, c):
             peer, slot, _, _, _ = z_plan(i)
-            device = {"gz": peer}
-            body = remote(
-                xe.at[own, DEPTH:top, chunk(c), :], xe.at[slot, DEPTH:top, chunk(c), :],
-                zsend.at[i, c], zrecv.at[i, c], device,
-            )
-            if c != 0:
-                return [body]
-            return [
-                remote(lt.at[own, 0], lt.at[slot, 0], zsend.at[i, nch], zrecv.at[i, nch], device),
-                body,
-            ]
-
-        def y_copies(i, slot, up, c, tile):
+            lo, hi = pieces[part]
+            at = part * nch + c
+            return remote(
+                xe.at[own, lo:hi, chunk(c), :], xe.at[slot, lo:hi, chunk(c), :],
+                zsend.at[i, at], zrecv.at[i, at], {"gz": peer},
+            )
+
+        def z_tile(i):
+            peer, slot, _, _, _ = z_plan(i)
+            return remote(
+                lt.at[own, 0], lt.at[slot, 0],
+                zsend.at[i, 3 * nch], zrecv.at[i, 3 * nch], {"gz": peer},
+            )
+
+        def z_rim(i):
+            peer, slot, _, _, _ = z_plan(i)
+            return remote(
+                xm.at[own], xm.at[slot],
+                zsend.at[i, 3 * nch + 1], zrecv.at[i, 3 * nch + 1], {"gz": peer},
+            )
+
+        def y_copy(i, slot, up, c):
             src = (top - DEPTH, top) if up else (DEPTH, 2 * DEPTH)
             dst = (0, DEPTH) if up else (top, ext)
-            device = {"gy": y + 1 if up else y - 1}
             at = 0 if c is None else c
-            copies = [
-                remote(
-                    xe.at[slot, src[0] : src[1], chunk(c), :],
-                    xe.at[slot, dst[0] : dst[1], chunk(c), :],
-                    ysend.at[i, up, at], yrecv.at[i, up, at], device,
-                )
-            ]
-            if tile:
-                copies.insert(
-                    0,
-                    remote(
-                        lt.at[slot, 0], lt.at[slot, 1 if up else 2],
-                        ysend.at[i, up, nch], yrecv.at[i, up, nch], device,
-                    ),
-                )
-            return copies
-
-        def x_copies(i, slot, side, c, tile):
-            device = {"gx": x + 1 if side else x - 1}
-            at = 0 if c is None else c
-            copies = [
-                remote(
-                    xs.at[slot, chunk(c), :], xr.at[side, slot, chunk(c), :],
-                    xsend.at[i, side, at], xrecv.at[i, side, at], device,
-                )
-            ]
-            if tile:
-                copies.insert(
-                    0,
-                    remote(
-                        lp.at[slot], lr.at[side, slot],
-                        xsend.at[i, side, nch], xrecv.at[i, side, nch], device,
-                    ),
-                )
-            return copies
+            return remote(
+                xe.at[slot, src[0] : src[1], chunk(c), :],
+                xe.at[slot, dst[0] : dst[1], chunk(c), :],
+                ysend.at[i, up, at], yrecv.at[i, up, at], {"gy": y + 1 if up else y - 1},
+            )
+
+        def y_tile(i, slot, up):
+            return remote(
+                lt.at[slot, 0], lt.at[slot, 1 if up else 2],
+                ysend.at[i, up, nch], yrecv.at[i, up, nch], {"gy": y + 1 if up else y - 1},
+            )
+
+        def x_copy(side, j):
+            return remote(
+                xs, xr.at[side, j], xsend.at[side, j], xrecv.at[side, j],
+                {"gx": x + 1 if side else x - 1, "gy": y + (1 - j)},
+            )
 
         has_low, has_high = y > 0, y < ny - 1
         ysends = (has_low, has_high)
         xsends = (x > 0, x < nx - 1)
 
-        def start(copies):
-            for copy in copies:
-                copy.start()
-
-        def wait_send(copies):
-            for copy in copies:
-                copy.wait_send()
-
-        def wait_recv(copies):
-            for copy in copies:
-                copy.wait_recv()
-
-        def both(sends, make, action, mirrored=False):
-            for side in (1, 0):
-                pl.when(sends[1 - side if mirrored else side])(
-                    lambda side=side: action(make(side))
-                )
-
-        for c in range(nch):
+        def y_each(action, make):
+            for up in (1, 0):
+                pl.when(ysends[up])(lambda up=up: action(make(up)))
+
+        def y_arrive(make):
+            for up in (1, 0):
+                pl.when(ysends[1 - up])(lambda up=up: make(up).wait_recv())
+
+        def x_each(action):
+            for j in (1, 0, 2):
+                for side in (0, 1):
+                    there = xsends[side] if j == 1 else xsends[side] & ysends[1 - j // 2]
+                    pl.when(there)(lambda side=side, j=j: action(x_copy(side, j)))
+
+        def begin(copy):
+            copy.start()
+
+        def z_start(make):
             for i in range(noff):
-                when(z_plan(i)[3], lambda i=i, c=c: start(z_copies(i, c)))
-            if c == 0:
-                both(ysends, lambda up: y_copies(noff, own, up, None, True), start)
+                when(z_plan(i)[3], lambda i=i: make(i).start())
+
+        z_start(z_tile)
+        z_start(lambda i: z_copy(i, 0, 0))
+        z_start(lambda i: z_copy(i, 1, 0))
+        for c in range(groups):
+            xs[c * 8 : c * 8 + 8, :] = gather_edges(
+                lambda r: xe[own, r, c * 8 : c * 8 + 8, :], DEPTH, top
+            )
+        xs[leads:lead8] = gather_edges(
+            lambda r: jnp.broadcast_to(lt[own, 0, r - DEPTH : r - DEPTH + 1, :], (8, cols)),
+            DEPTH, top,
+        )
+        x_each(begin)
+        y_each(begin, lambda up: y_copy(noff, own, up, None))
+        y_each(begin, lambda up: y_tile(noff, own, up))
+        for c in range(1, nch):
+            for part in (0, 1):
+                z_start(lambda i: z_copy(i, part, c))
+        for c in range(nch - 1):
+            z_start(lambda i: z_copy(i, 2, c))
 
         eye = lax.broadcasted_iota(jnp.int32, (leads, leads), 0) == lax.broadcasted_iota(
             jnp.int32, (leads, leads), 1
@@ -250,82 +283,58 @@
             )
             elec[e] = jnp.broadcast_to(column, (leads, cols))
 
-        def group(c):
-            return pl.ds(pl.multiple_of(c * 8, 8), 8)
-
-        lane = lax.broadcasted_iota(jnp.int32, (8, cols), 1)
-
-        def gather_edges(load):
-            total = jnp.zeros((8, cols), jnp.float32)
-            for r in range(ext):
-                moved = pltpu.roll(load(r), 8 * r, axis=1) if r else load(r)
-                if r == 0:
-                    keep = (lane < DEPTH) | (lane >= cols - DEPTH)
-                else:
-                    keep = (lane >= 8 * r - DEPTH) & (lane < 8 * r + DEPTH)
-                total = jnp.where(keep, moved, total)
-            return total
-
-        def pack(slot, lo, hi):
-            def step(c, _):
-                xs[slot, group(c), :] = gather_edges(lambda r: xe[slot, r, group(c), :])
-                return 0
-
-            lax.fori_loop(lo, hi, step, 0)
-
-        def pack_labels(slot):
+        near = (lane & 7) < 4
+        middle = (lane >= 8 * DEPTH - DEPTH) & (lane < 8 * top - DEPTH)
+
+        def forward(c):
+            for part in (0, 1):
+                for i in range(noff):
+
+                    def arrived(i=i, part=part):
+                        z_copy(i, part, c).wait_recv()
+                        pl.when(ysends[part])(
+                            lambda: y_copy(i, z_plan(i)[2], part, c).start()
+                        )
+
+                    when(z_plan(i)[4], arrived)
+
+        for i in range(noff):
+
+            def arrived(i=i):
+                z_tile(i).wait_recv()
+                y_each(begin, lambda up: y_tile(i, z_plan(i)[2], up))
+
+            when(z_plan(i)[4], arrived)
+        forward(0)
+
+        for side in (0, 1):
+            for j in range(3):
+                pl.when(exists(side, j))(lambda side=side, j=j: x_copy(side, j).wait_recv())
+
+        for c in range(lead8 // 8):
+            at = slice(c * 8, c * 8 + 8)
+            sides = [jnp.where(near, xr[0, j, at, :], xr[1, j, at, :]) for j in range(3)]
+            corners = jnp.where(lane < 8 * DEPTH + 28, sides[2], sides[0])
+            xm[own, at, :] = jnp.where(middle, sides[1], pltpu.roll(corners, 8 * rows, axis=1))
+
+        z_start(z_rim)
+        z_start(lambda i: z_copy(i, 2, nch - 1))
+        for c in range(1, nch):
+            forward(c)
+
+        y_arrive(lambda up: y_tile(noff, own, up))
+        for i in range(noff):
+            when(z_plan(i)[4], lambda i=i: y_arrive(lambda up: y_tile(i, z_plan(i)[2], up)))
+
+        for s in range(layers):
             for r in range(ext):
                 if r < DEPTH:
-                    row = lt[slot, 1, rows - DEPTH + r : rows - DEPTH + r + 1, :]
+                    row = lt[s, 1, rows - DEPTH + r : rows - DEPTH + r + 1, :]
                 elif r < top:
-                    row = lt[slot, 0, r - DEPTH : r - DEPTH + 1, :]
+                    row = lt[s, 0, r - DEPTH : r - DEPTH + 1, :]
                 else:
-                    row = lt[slot, 2, r - top : r - top + 1, :]
-                lab[slot, r] = jnp.broadcast_to(row, (8, cols))
-            lp[slot] = gather_edges(lambda r: lab[slot, r])
-
-        def forward_y(c):
-            for i in range(noff):
-
-                def arrived(i=i):
-                    wait_recv(z_copies(i, c))
-                    slot = z_plan(i)[2]
-                    both(ysends, lambda up: y_copies(i, slot, up, c, c == 0), start)
-
-                when(z_plan(i)[4], arrived)
-
-        def forward_x(c):
-            tile = isinstance(c, int) and c == 0
-            for i in range(noff):
-                slot = z_plan(i)[2]
-
-                def arrived(i=i, slot=slot):
-                    make = lambda up: y_copies(i, slot, up, c, tile)
-                    both(ysends, make, wait_recv, mirrored=True)
-
-                when(z_plan(i)[4], arrived)
-                if tile:
-                    pack_labels(slot)
-                pack(slot, c * per, (c + 1) * per)
-                both(xsends, lambda side: x_copies(i, slot, side, c, tile), start)
-
-        both(ysends, lambda up: y_copies(noff, own, up, None, True), wait_recv, mirrored=True)
-        pack_labels(own)
-        pack(own, 0, groups)
-        both(xsends, lambda side: x_copies(noff, own, side, None, True), start)
-
-        forward_y(0)
-        for c in range(1, nch):
-            forward_y(c)
-            if c <= nch - 2:
-                forward_x(c - 1)
-
-        both(xsends, lambda side: x_copies(noff, own, side, None, True), wait_recv, mirrored=True)
-        for i in range(noff):
-            slot = z_plan(i)[2]
-            both(
-                xsends, lambda side: x_copies(i, slot, side, 0, True)[:1], wait_recv, mirrored=True
-            )
+                    row = lt[s, 2, r - top : r - top + 1, :]
+                lab[s, r] = jnp.broadcast_to(row, (8, cols))
 
         values = [[table[i, t] for t in range(table.shape[1])] for i in range(6)]
 
@@ -335,8 +344,6 @@
                 match = label == float(t)
                 parts = [jnp.where(match, values[i][t], parts[i]) for i in range(6)]
             return parts, jnp.where(label >= 0.0, 1.0, 0.0)
-
-        near = (lane & 7) < 4
 
         def lookup(r, _):
             for s in range(layers):
@@ -347,10 +354,15 @@
             return 0
 
         lax.fori_loop(0, ext, lookup, 0)
+        edges = [gather_edges(lambda r: lab[s, r], 0, ext) for s in range(layers)]
+        y_arrive(lambda up: y_copy(noff, own, up, None))
+        for i in range(noff):
+            when(z_plan(i)[4], lambda i=i: z_rim(i).wait_recv())
         for s in range(layers):
             for side in (0, 1):
+                beyond = xm[s, leads:lead8, :]
                 label = (
-                    jnp.where(near, lp[s], lr[1, s]) if side else jnp.where(near, lr[0, s], lp[s])
+                    jnp.where(near, edges[s], beyond) if side else jnp.where(near, beyond, edges[s])
                 )
                 parts, here = look(label)
                 for i in range(6):
@@ -406,38 +418,51 @@
                 for s in range(layers)
             ]
 
-        def operate(load, emit, lo, hi, joins):
-            below_y = [None] * layers
+        def operate(load, emit, lo, hi, joins, count):
+            below_y = [[None] * layers for _ in range(count)]
             for r in range(lo - 1, hi):
-                here = [load(s, r) for s in range(layers)]
-                below_z = None
+                here = [[load(k, s, r) for s in range(layers)] for k in range(count)]
+                below_z = [None] * count
                 for s in range(layers):
                     t = [coef[i, s, r] for i in range(6)]
-                    v = here[s]
-                    join = pltpu.roll(joins[s], (cols + 1 - 8 * r) % cols, axis=1)
-                    grads = (
-                        jnp.where(ends[1], join, pltpu.roll(v, last, axis=1)) - v,
-                        load(s, r + 1) - v,
-                        here[s + 1] - v if s + 1 < layers else -v,
-                    )
-                    flux_y = flux(t, 1, grads)
-                    if r >= lo:
-                        flux_x, flux_z = flux(t, 0, grads), flux(t, 2, grads)
-                        before = jnp.where(ends[0], join, pltpu.roll(flux_x, 1, axis=1))
-                        total = (below_y[s] - flux_y) + (before - flux_x)
-                        total = total - flux_z if below_z is None else total + (below_z - flux_z)
-                        emit(s, r, total)
-                        below_z = flux_z
-                    below_y[s] = flux_y
-
-        def advance(c):
-            mine = [xs[s, group(c), :] for s in range(layers)]
-            right = [jnp.where(near, xr[0, s, group(c), :], mine[s]) for s in range(layers)]
-            left = [jnp.where(near, mine[s], xr[1, s, group(c), :]) for s in range(layers)]
+                    for k in range(count):
+                        v = here[k][s]
+                        join = pltpu.roll(joins[k][s], (cols + 1 - 8 * r) % cols, axis=1)
+                        grads = (
+                            jnp.where(ends[1], join, pltpu.roll(v, last, axis=1)) - v,
+                            load(k, s, r + 1) - v,
+                            here[k][s + 1] - v if s + 1 < layers else -v,
+                        )
+                        flux_y = flux(t, 1, grads)
+                        if r >= lo:
+                            flux_x, flux_z = flux(t, 0, grads), flux(t, 2, grads)
+                            before = jnp.where(ends[0], join, pltpu.roll(flux_x, 1, axis=1))
+                            total = (below_y[k][s] - flux_y) + (before - flux_x)
+                            total = total - flux_z if s == 0 else total + (below_z[k] - flux_z)
+                            emit(k, s, r, total)
+                            below_z[k] = flux_z
+                        below_y[k][s] = flux_y
+
+        def clip(value, s, r):
+            return value if not windowed and DEPTH <= r < top else value * inside[s, r]
+
+        plane_voxels = ny * rows * line_width
+
+        def rims(c):
+            mine = [
+                gather_edges(lambda r: xe[s, r, group(c), :], 0, ext) for s in range(layers)
+            ]
+            beyond = [xm[s, group(c), :] for s in range(layers)]
+            right = [jnp.where(near, beyond[s], mine[s]) for s in range(layers)]
+            left = [jnp.where(near, mine[s], beyond[s]) for s in range(layers)]
+
+            def keep(n, joins):
+                for s in range(layers):
+                    joined[n, s, group(c), :] = joins[s]
+
             right_sum, _ = rim(right, 0, True)
             left_sum, left_edge = rim(left, 1, True)
-            joins_v = seams(right, left_edge)
-            plane_voxels = ny * rows * line_width
+            keep(0, seams(right, left_edge))
 
             def rim_r(total, s, side):
                 voxel = packed_voxel + ((first + s) * plane_voxels + (0 if side else cols))
@@ -447,49 +472,63 @@
             left_r = [rim_r(left_sum[s], s, 1) for s in range(layers)]
             right_sum, _ = rim(right_r, 0, True)
             left_sum, left_edge = rim(left_r, 1, True)
-            joins_r = seams(right_r, left_edge)
+            keep(1, seams(right_r, left_edge))
             right_q = [right_sum[s] * hinside[s, 0] for s in range(layers)]
             left_q = [left_sum[s] * hinside[s, 1] for s in range(layers)]
             _, left_edge = rim(left_q, 1, False)
-            joins_q = seams(right_q, left_edge)
-
-            def emit_r(s, r, total):
+            keep(2, seams(right_q, left_edge))
+
+        def advance(cs):
+            def joins_of(n, c):
+                return [joined[n, s, group(c), :] for s in range(layers)]
+
+            def emit_r(k, s, r, total):
                 row = (first + s) * (ny * rows) + y * rows + (r - DEPTH)
                 voxel = column + (row * line_width).astype(jnp.float32)
-                re[s, r] = (source(c, voxel) - total) * inside[s, r]
-
-            def emit_q(s, r, total):
-                qe[s, r] = total * inside[s, r]
-
-            def emit_p(s, r, total):
-                pe[s, r - DEPTH] = total
-
-            operate(lambda s, r: xe[s, r, group(c), :], emit_r, 1, ext - 1, joins_v)
-            operate(lambda s, r: re[s, r], emit_q, 2, ext - 2, joins_r)
-            operate(lambda s, r: qe[s, r], emit_p, 3, ext - 3, joins_q)
-            for r in range(rows):
-                at = slice(r * cols, (r + 1) * cols)
-                base_out[group(c), at] = re[own, DEPTH + r]
-                base_out[group(c + groups), at] = qe[own, DEPTH + r]
-                base_out[group(c + 2 * groups), at] = pe[own, r]
+                re[k, s, r] = clip(source(cs[k], voxel) - total, s, r)
+
+            def emit_q(k, s, r, total):
+                qe[k, s, r] = clip(total, s, r)
+
+            def emit_p(k, s, r, total):
+                pe[k, s, r - DEPTH] = total
+
+            def field_of(k, s, r):
+                return xe[s, r, group(cs[k]), :]
+
+            count = len(cs)
+            joins = [[joins_of(n, c) for c in cs] for n in range(3)]
+            operate(field_of, emit_r, 1, ext - 1, joins[0], count)
+            operate(lambda k, s, r: re[k, s, r], emit_q, 2, ext - 2, joins[1], count)
+            operate(lambda k, s, r: qe[k, s, r], emit_p, 3, ext - 3, joins[2], count)
+            for k, c in enumerate(cs):
+                for r in range(rows):
+                    at = slice(r * cols, (r + 1) * cols)
+                    base_out[group(c), at] = re[k, own, DEPTH + r]
+                    base_out[group(c + groups), at] = qe[k, own, DEPTH + r]
+                    base_out[group(c + 2 * groups), at] = pe[k, own, r]
 
         def turn(c, _):
-            @pl.when(c < 2)
-            def _():
-                forward_x(c + (nch - 2))
-
             for i in range(noff):
-                slot = z_plan(i)[2]
-                both(
-                    xsends, lambda side: x_copies(i, slot, side, c, False), wait_recv,
-                    mirrored=True,
-                )
+
+                def arrived(i=i):
+                    z_copy(i, 2, c).wait_recv()
+                    y_arrive(lambda up: y_copy(i, z_plan(i)[2], up, c))
+
+                when(z_plan(i)[4], arrived)
+
+            def edge(g, _):
+                for k in range(TWIN):
+                    rims(c * per + g * TWIN + k)
+                return 0
+
+            lax.fori_loop(0, per // TWIN, edge, 0)
 
             def step(g, _):
-                advance(c * per + g)
+                advance([c * per + g * PAIR + k for k in range(PAIR)])
                 return 0
 
-            lax.fori_loop(0, per, step, 0)
+            lax.fori_loop(0, per // PAIR, step, 0)
             return 0
 
         lax.fori_loop(0, nch, turn, 0)
@@ -497,7 +536,7 @@
         upper = nt_dot(base_out[0:leads, :], base_out[0 : 2 * leads, :])
         lower = nt_dot(base_out[leads : 2 * leads, :], base_out[leads : 3 * leads, :])
         grams = jnp.concatenate([upper, lower], axis=0)
-        for i in range(owners):
+        for i in range(plane):
             gs[i] = grams[i * share : (i + 1) * share, :]
 
         save = pltpu.make_async_copy(base_out, base_hbm, ssem.at[0])
@@ -509,49 +548,55 @@
                 for k, (pid, device) in enumerate(peers)
                 if k
             ]
-            start(copies)
+            for copy in copies:
+                copy.start()
             for copy in copies:
                 copy.wait()
 
-        peers = all_peers if flat else plane_peers
-        me = peers[0][0]
+        me = plane_peers[0][0]
         rs[me] = gs[me]
-        exchange(0, peers, lambda pid: gs.at[pid], rs.at[me])
-        if flat:
-            total[...] = jnp.sum(rs[...], axis=0)
-        else:
-            zs[x] = jnp.sum(rs[...], axis=0)
-            exchange(1, line_peers, lambda pid: zs.at[x], zs.at[x])
-            total[...] = jnp.sum(zs[...], axis=0)
+        exchange(0, plane_peers, lambda pid: gs.at[pid], rs.at[me])
+        zs[x] = jnp.sum(rs[...], axis=0)
+        exchange(1, line_peers, lambda pid: zs.at[x], zs.at[x])
+        total[...] = jnp.sum(zs[...], axis=0)
         keep = pltpu.make_async_copy(total, gram_hbm.at[me], ssem.at[1])
         keep.start()
-        exchange(2, peers, lambda pid: total, gram_hbm.at[me])
+        exchange(2, plane_peers, lambda pid: total, gram_hbm.at[me])
         keep.wait()
         save.wait()
 
-        both(ysends, lambda up: y_copies(noff, own, up, None, True), wait_send)
-        both(xsends, lambda side: x_copies(noff, own, side, None, True), wait_send)
+        def sent(copy):
+            copy.wait_send()
+
+        y_each(sent, lambda up: y_copy(noff, own, up, None))
+        y_each(sent, lambda up: y_tile(noff, own, up))
+        x_each(sent)
         for i in range(noff):
-            slot = z_plan(i)[2]
-            for c in range(nch):
-                when(z_plan(i)[3], lambda i=i, c=c: wait_send(z_copies(i, c)))
-
-                def sent(i=i, slot=slot, c=c):
-                    both(ysends, lambda up: y_copies(i, slot, up, c, c == 0), wait_send)
-
-                when(z_plan(i)[4], sent)
-                both(xsends, lambda side: x_copies(i, slot, side, c, c == 0), wait_send)
+            for part in range(3):
+                for c in range(nch):
+                    when(z_plan(i)[3], lambda i=i, part=part, c=c: sent(z_copy(i, part, c)))
+            when(z_plan(i)[3], lambda i=i: sent(z_tile(i)))
+            when(z_plan(i)[3], lambda i=i: sent(z_rim(i)))
+
+            def forwarded(i=i):
+                slot = z_plan(i)[2]
+                for c in range(nch):
+                    y_each(sent, lambda up: y_copy(i, slot, up, c))
+                y_each(sent, lambda up: y_tile(i, slot, up))
+
+            when(z_plan(i)[4], forwarded)
 
     f32 = jnp.float32
     tile = (8, cols)
-    group_sems = pltpu.SemaphoreType.DMA((3, max(owners, nx)))
+    group_sems = pltpu.SemaphoreType.DMA((3, max(plane, nx)))
     y_sems = pltpu.SemaphoreType.DMA((noff + 1, 2, nch + 1))
-    z_sems = pltpu.SemaphoreType.DMA((noff, nch + 1))
+    z_sems = pltpu.SemaphoreType.DMA((noff, 3 * nch + 2))
+    x_sems = pltpu.SemaphoreType.DMA((2, 3))
     call = pl.pallas_call(
         kernel,
         out_shape=(
             jax.ShapeDtypeStruct((3 * leads, rows * cols), f32),
-            jax.ShapeDtypeStruct((owners, share, size), f32),
+            jax.ShapeDtypeStruct((plane, share, size), f32),
         ),
         in_specs=[pl.BlockSpec(memory_space=pltpu.HBM)] * 4,
         out_specs=[pl.BlockSpec(memory_space=pltpu.HBM)] * 2,
@@ -567,22 +612,22 @@
             pltpu.VMEM((layers, ext, leads, cols), f32),
             pltpu.VMEM((layers, 3) + tile, f32),
             pltpu.VMEM((layers, ext) + tile, f32),
-            pltpu.VMEM((layers,) + tile, f32),
-            pltpu.VMEM((2, layers) + tile, f32),
-            pltpu.VMEM((layers, leads, cols), f32),
-            pltpu.VMEM((2, layers, leads, cols), f32),
-            pltpu.VMEM((layers, ext) + tile, f32),
-            pltpu.VMEM((layers, ext) + tile, f32),
-            pltpu.VMEM((layers, rows) + tile, f32),
+            pltpu.VMEM((lead8, cols), f32),
+            pltpu.VMEM((2, 3, lead8, cols), f32),
+            pltpu.VMEM((layers, lead8, cols), f32),
+            pltpu.VMEM((3, layers, leads, cols), f32),
+            pltpu.VMEM((PAIR, layers, ext) + tile, f32),
+            pltpu.VMEM((PAIR, layers, ext) + tile, f32),
+            pltpu.VMEM((PAIR, layers, rows) + tile, f32),
             pltpu.VMEM((6, layers, ext) + tile, f32),
             pltpu.VMEM((layers, ext) + tile, f32),
             pltpu.VMEM((6, layers, 2) + tile, f32),
             pltpu.VMEM((layers, 2) + tile, f32),
             pltpu.VMEM((2, leads, cols), f32),
-            pltpu.VMEM((owners, share, size), f32),
-            pltpu.VMEM((owners, share, size), f32),
+            pltpu.VMEM((plane, share, size), f32),
+            pltpu.VMEM((plane, share, size), f32),
             pltpu.VMEM((nx, share, size), f32),
-            z_sems, z_sems, y_sems, y_sems, y_sems, y_sems, group_sems, group_sems,
+            z_sems, z_sems, y_sems, y_sems, x_sems, x_sems, group_sems, group_sems,
         ],
         compiler_params=pltpu.CompilerParams(
             collective_id=0, has_side_effects=True,

time: 43.3 us -> 39 us (0.901)
  Pallas kernels: 42.5 us -> 38.2 us
    pallas_call x1, Pallas kernels: 35.2 us -> 30.9 us  [body(): krylov(tissue_tensors, labels.reshape(rows, cols), electrodes, field)]
where the time goes in v2:
time: 39 us; the launch traced here: 38.8 us
  Pallas kernels  38.2 us (98%)
  between operations  0.64 us (2%)
    pallas_call x1, Pallas kernels, body(): krylov(tissue_tensors, labels.reshape(rows, cols), electrodes, field)  30.9 us
    pallas_call x1, Pallas kernels, body(): make_combine(leads, rows, cols)(gram.reshape(size, size), base, field)  7.32 us

profile of v2, /device:TPU:0, one launch (start us, length us, event | category | flops | bytes accessed | tf_op | source)
XLA Modules:
  0.0 38.8 jit_solution(15925894111640951994)
XLA Ops:
  0.6 30.9 %krylov.1 = (f32[192,1024]{1,0:T(8,128)}, f32[8,16,128]{2,1,0:T(8,128)}) custom-call(f32[6,8]{1,0:T(8,128)} %table_hbm.1, s32[8,128]{1,0:T(8,128)} %bitcast.12, s32[2,64]{1,0:T(2,128)} %electrodes_hbm.1, f32[512,128]{1,0:T(8,128)} %bitcast.9), custom_call_target="tpu_custom_call" | custom-call | tf_op jit(solution)/shard_map/krylov/pallas_call | solution.py:793
  31.5 7.3 %combine.1 = (f32[512,128]{1,0:T(8,128)}, f32[512,128]{1,0:T(8,128)}) custom-call(f32[128,128]{1,0:T(8,128)} %bitcast.11, f32[192,1024]{1,0:T(8,128)} %get-tuple-element.7.base_hbm, f32[512,128]{1,0:T(8,128)} %bitcast.10), custom_call_target="tpu_custom_call" | custom-call | tf_op jit(solution)/shard_map/combine/pallas_call | solution.py:794

commit v3 on v2

--- a/solution.py
+++ b/solution.py
@@ -8,9 +8,9 @@
 MESH = pl.DeviceIdType.MESH
 HIGH = lax.Precision.HIGHEST
 DEPTH = 3
-CHUNKS = 2
-PAIR = 1
-TWIN = 4
+CHUNKS = 4
+PAIR = 2
+TWIN = 2
 VMEM_LIMIT = 58 * 1024 * 1024
 
 
@@ -49,7 +49,7 @@
     def kernel(
         table_hbm, labels_hbm, electrodes_hbm, field_hbm, base_hbm, gram_hbm,
         base_out, total, ssem, table, labels, electrodes, field, lsem,
-        xe, lt, lab, xs, xr, xm, joined, re, qe, pe, coef, inside, hcoef, hinside, elec, gs, rs, zs,
+        xe, lt, lab, lp, xs, xr, xm, xp, xq, joined, re, qe, pe, coef, inside, hcoef, hinside, elec, gs, rs, zs,
         zsend, zrecv, ysend, yrecv, xsend, xrecv, asend, arecv,
     ):
         z, y, x = lax.axis_index("gz"), lax.axis_index("gy"), lax.axis_index("gx")
@@ -270,7 +270,7 @@
         for c in range(1, nch):
             for part in (0, 1):
                 z_start(lambda i: z_copy(i, part, c))
-        for c in range(nch - 1):
+        for c in range(nch // 2):
             z_start(lambda i: z_copy(i, 2, c))
 
         eye = lax.broadcasted_iota(jnp.int32, (leads, leads), 0) == lax.broadcasted_iota(
@@ -307,35 +307,6 @@
             when(z_plan(i)[4], arrived)
         forward(0)
 
-        for side in (0, 1):
-            for j in range(3):
-                pl.when(exists(side, j))(lambda side=side, j=j: x_copy(side, j).wait_recv())
-
-        for c in range(lead8 // 8):
-            at = slice(c * 8, c * 8 + 8)
-            sides = [jnp.where(near, xr[0, j, at, :], xr[1, j, at, :]) for j in range(3)]
-            corners = jnp.where(lane < 8 * DEPTH + 28, sides[2], sides[0])
-            xm[own, at, :] = jnp.where(middle, sides[1], pltpu.roll(corners, 8 * rows, axis=1))
-
-        z_start(z_rim)
-        z_start(lambda i: z_copy(i, 2, nch - 1))
-        for c in range(1, nch):
-            forward(c)
-
-        y_arrive(lambda up: y_tile(noff, own, up))
-        for i in range(noff):
-            when(z_plan(i)[4], lambda i=i: y_arrive(lambda up: y_tile(i, z_plan(i)[2], up)))
-
-        for s in range(layers):
-            for r in range(ext):
-                if r < DEPTH:
-                    row = lt[s, 1, rows - DEPTH + r : rows - DEPTH + r + 1, :]
-                elif r < top:
-                    row = lt[s, 0, r - DEPTH : r - DEPTH + 1, :]
-                else:
-                    row = lt[s, 2, r - top : r - top + 1, :]
-                lab[s, r] = jnp.broadcast_to(row, (8, cols))
-
         values = [[table[i, t] for t in range(table.shape[1])] for i in range(6)]
 
         def look(label):
@@ -345,24 +316,86 @@
                 parts = [jnp.where(match, values[i][t], parts[i]) for i in range(6)]
             return parts, jnp.where(label >= 0.0, 1.0, 0.0)
 
-        def lookup(r, _):
-            for s in range(layers):
-                parts, here = look(lab[s, r])
-                for i in range(6):
-                    coef[i, s, r] = parts[i]
-                inside[s, r] = here
+        def prepare(slot, c):
+            xp[slot, group(c), :] = gather_edges(lambda r: xe[slot, r, group(c), :], 0, ext)
+            for r in range(ext - 1):
+                xq[slot, r, group(c), :] = pltpu.roll(xe[slot, r, group(c), :], last, axis=1)
+
+        def prepare_own(c, _):
+            prepare(own, c * 2)
+            prepare(own, c * 2 + 1)
             return 0
 
-        lax.fori_loop(0, ext, lookup, 0)
-        edges = [gather_edges(lambda r: lab[s, r], 0, ext) for s in range(layers)]
+        def label_rows(slot):
+            for r in range(ext):
+                if r < DEPTH:
+                    row = lt[slot, 1, rows - DEPTH + r : rows - DEPTH + r + 1, :]
+                elif r < top:
+                    row = lt[slot, 0, r - DEPTH : r - DEPTH + 1, :]
+                else:
+                    row = lt[slot, 2, r - top : r - top + 1, :]
+                lab[slot, r] = jnp.broadcast_to(row, (8, cols))
+            lp[slot] = gather_edges(lambda r: lab[slot, r], 0, ext)
+
+            def lookup(n, _):
+                for r in (n * 2, n * 2 + 1):
+                    parts, here = look(lab[slot, r])
+                    for i in range(6):
+                        coef[i, slot, r] = parts[i]
+                    inside[slot, r] = here
+                return 0
+
+            lax.fori_loop(0, ext // 2, lookup, 0)
+
+        for side in (0, 1):
+            for j in range(3):
+                pl.when(exists(side, j))(lambda side=side, j=j: x_copy(side, j).wait_recv())
+
+        for c in range(lead8 // 8):
+            at = slice(c * 8, c * 8 + 8)
+            sides = [jnp.where(near, xr[0, j, at, :], xr[1, j, at, :]) for j in range(3)]
+            corners = jnp.where(lane < 8 * DEPTH + 28, sides[2], sides[0])
+            xm[own, at, :] = jnp.where(middle, sides[1], pltpu.roll(corners, 8 * rows, axis=1))
+
+        z_start(z_rim)
+        for c in range(nch // 2, nch):
+            z_start(lambda i: z_copy(i, 2, c))
+        y_arrive(lambda up: y_tile(noff, own, up))
+        label_rows(own)
         y_arrive(lambda up: y_copy(noff, own, up, None))
+        lax.fori_loop(0, groups // 2, prepare_own, 0)
+
+        for c in range(1, nch):
+            forward(c)
+
+        for i in range(noff):
+            when(z_plan(i)[4], lambda i=i: y_arrive(lambda up: y_tile(i, z_plan(i)[2], up)))
+            label_rows(z_plan(i)[2])
+
+        def ready(c):
+            for i in range(noff):
+
+                def arrived(i=i):
+                    z_copy(i, 2, c).wait_recv()
+                    y_arrive(lambda up: y_copy(i, z_plan(i)[2], up, c))
+
+                when(z_plan(i)[4], arrived)
+
+            def step(g, _):
+                for i in range(noff):
+                    prepare(z_plan(i)[2], c * per + g)
+                return 0
+
+            lax.fori_loop(0, per, step, 0)
+
+        ready(0)
         for i in range(noff):
             when(z_plan(i)[4], lambda i=i: z_rim(i).wait_recv())
         for s in range(layers):
             for side in (0, 1):
                 beyond = xm[s, leads:lead8, :]
                 label = (
-                    jnp.where(near, edges[s], beyond) if side else jnp.where(near, beyond, edges[s])
+                    jnp.where(near, lp[s], beyond) if side else jnp.where(near, beyond, lp[s])
                 )
                 parts, here = look(label)
                 for i in range(6):
@@ -418,8 +451,10 @@
                 for s in range(layers)
             ]
 
-        def operate(load, emit, lo, hi, joins, count):
+        def operate(load, emit, lo, hi, joins, count, shifted=None):
             below_y = [[None] * layers for _ in range(count)]
+            if shifted is None:
+                shifted = lambda k, s, r, v: pltpu.roll(v, last, axis=1)
             for r in range(lo - 1, hi):
                 here = [[load(k, s, r) for s in range(layers)] for k in range(count)]
                 below_z = [None] * count
@@ -429,7 +464,7 @@
                         v = here[k][s]
                         join = pltpu.roll(joins[k][s], (cols + 1 - 8 * r) % cols, axis=1)
                         grads = (
-                            jnp.where(ends[1], join, pltpu.roll(v, last, axis=1)) - v,
+                            jnp.where(ends[1], join, shifted(k, s, r, v)) - v,
                             load(k, s, r + 1) - v,
                             here[k][s + 1] - v if s + 1 < layers else -v,
                         )
@@ -449,9 +484,7 @@
         plane_voxels = ny * rows * line_width
 
         def rims(c):
-            mine = [
-                gather_edges(lambda r: xe[s, r, group(c), :], 0, ext) for s in range(layers)
-            ]
+            mine = [xp[s, group(c), :] for s in range(layers)]
             beyond = [xm[s, group(c), :] for s in range(layers)]
             right = [jnp.where(near, beyond[s], mine[s]) for s in range(layers)]
             left = [jnp.where(near, mine[s], beyond[s]) for s in range(layers)]
@@ -478,44 +511,49 @@
             _, left_edge = rim(left_q, 1, False)
             keep(2, seams(right_q, left_edge))
 
-        def advance(cs):
-            def joins_of(n, c):
-                return [joined[n, s, group(c), :] for s in range(layers)]
-
-            def emit_r(k, s, r, total):
+        def joins_of(n, cs):
+            return [[joined[n, s, group(c), :] for s in range(layers)] for c in cs]
+
+        def apply_r(cs):
+            def emit(k, s, r, total):
                 row = (first + s) * (ny * rows) + y * rows + (r - DEPTH)
                 voxel = column + (row * line_width).astype(jnp.float32)
-                re[k, s, r] = clip(source(cs[k], voxel) - total, s, r)
-
-            def emit_q(k, s, r, total):
-                qe[k, s, r] = clip(total, s, r)
-
-            def emit_p(k, s, r, total):
-                pe[k, s, r - DEPTH] = total
-
-            def field_of(k, s, r):
+                re[s, r, group(cs[k]), :] = clip(source(cs[k], voxel) - total, s, r)
+
+            def load(k, s, r):
                 return xe[s, r, group(cs[k]), :]
 
-            count = len(cs)
-            joins = [[joins_of(n, c) for c in cs] for n in range(3)]
-            operate(field_of, emit_r, 1, ext - 1, joins[0], count)
-            operate(lambda k, s, r: re[k, s, r], emit_q, 2, ext - 2, joins[1], count)
-            operate(lambda k, s, r: qe[k, s, r], emit_p, 3, ext - 3, joins[2], count)
-            for k, c in enumerate(cs):
+            def shifted(k, s, r, v):
+                return xq[s, r, group(cs[k]), :]
+
+            operate(load, emit, 1, ext - 1, joins_of(0, cs), len(cs), shifted)
+
+        def apply_q(cs):
+            def emit(k, s, r, total):
+                qe[s, r, group(cs[k]), :] = clip(total, s, r)
+
+            def load(k, s, r):
+                return re[s, r, group(cs[k]), :]
+
+            operate(load, emit, 2, ext - 2, joins_of(1, cs), len(cs))
+
+        def apply_p(cs):
+            def emit(k, s, r, total):
+                pe[s, r - DEPTH, group(cs[k]), :] = total
+
+            def load(k, s, r):
+                return qe[s, r, group(cs[k]), :]
+
+            operate(load, emit, 3, ext - 3, joins_of(2, cs), len(cs))
+            for c in cs:
                 for r in range(rows):
                     at = slice(r * cols, (r + 1) * cols)
-                    base_out[group(c), at] = re[k, own, DEPTH + r]
-                    base_out[group(c + groups), at] = qe[k, own, DEPTH + r]
-                    base_out[group(c + 2 * groups), at] = pe[k, own, r]
+                    base_out[group(c), at] = re[own, DEPTH + r, group(c), :]
+                    base_out[group(c + groups), at] = qe[own, DEPTH + r, group(c), :]
+                    base_out[group(c + 2 * groups), at] = pe[own, r, group(c), :]
 
         def turn(c, _):
-            for i in range(noff):
-
-                def arrived(i=i):
-                    z_copy(i, 2, c).wait_recv()
-                    y_arrive(lambda up: y_copy(i, z_plan(i)[2], up, c))
-
-                when(z_plan(i)[4], arrived)
+            pl.when(c > 0)(lambda: ready(c))
 
             def edge(g, _):
                 for k in range(TWIN):
@@ -524,17 +562,20 @@
 
             lax.fori_loop(0, per // TWIN, edge, 0)
 
-            def step(g, _):
-                advance([c * per + g * PAIR + k for k in range(PAIR)])
-                return 0
-
-            lax.fori_loop(0, per // PAIR, step, 0)
+            for apply, pair in ((apply_r, PAIR), (apply_q, PAIR), (apply_p, PAIR)):
+
+                def step(g, _, apply=apply, pair=pair):
+                    apply([c * per + g * pair + k for k in range(pair)])
+                    return 0
+
+                lax.fori_loop(0, per // pair, step, 0)
             return 0
 
         lax.fori_loop(0, nch, turn, 0)
 
-        upper = nt_dot(base_out[0:leads, :], base_out[0 : 2 * leads, :])
-        lower = nt_dot(base_out[leads : 2 * leads, :], base_out[leads : 3 * leads, :])
+        products = nt_dot(base_out[0 : 2 * leads, :], base_out[...])
+        upper = products[0:leads, 0 : 2 * leads]
+        lower = products[leads : 2 * leads, leads : 3 * leads]
         grams = jnp.concatenate([upper, lower], axis=0)
         for i in range(plane):
             gs[i] = grams[i * share : (i + 1) * share, :]
@@ -612,13 +653,16 @@
             pltpu.VMEM((layers, ext, leads, cols), f32),
             pltpu.VMEM((layers, 3) + tile, f32),
             pltpu.VMEM((layers, ext) + tile, f32),
+            pltpu.VMEM((layers,) + tile, f32),
             pltpu.VMEM((lead8, cols), f32),
             pltpu.VMEM((2, 3, lead8, cols), f32),
             pltpu.VMEM((layers, lead8, cols), f32),
+            pltpu.VMEM((layers, leads, cols), f32),
+            pltpu.VMEM((layers, ext - 1, leads, cols), f32),
             pltpu.VMEM((3, layers, leads, cols), f32),
-            pltpu.VMEM((PAIR, layers, ext) + tile, f32),
-            pltpu.VMEM((PAIR, layers, ext) + tile, f32),
-            pltpu.VMEM((PAIR, layers, rows) + tile, f32),
+            pltpu.VMEM((layers, ext, leads, cols), f32),
+            pltpu.VMEM((layers, ext, leads, cols), f32),
+            pltpu.VMEM((layers, rows, leads, cols), f32),
             pltpu.VMEM((6, layers, ext) + tile, f32),
             pltpu.VMEM((layers, ext) + tile, f32),
             pltpu.VMEM((6, layers, 2) + tile, f32),

time: 39 us -> 38.1 us (0.977)
  Pallas kernels: 38.2 us -> 37.3 us
    pallas_call x1, Pallas kernels: 30.9 us -> 30 us  [body(): krylov(tissue_tensors, labels.reshape(rows, cols), electrodes, field)]
where the time goes in v3:
time: 38.1 us; the launch traced here: 37.9 us
  Pallas kernels  37.3 us (98%)
  between operations  0.64 us (2%)
    pallas_call x1, Pallas kernels, body(): krylov(tissue_tensors, labels.reshape(rows, cols), electrodes, field)  30 us
    pallas_call x1, Pallas kernels, body(): make_combine(leads, rows, cols)(gram.reshape(size, size), base, field)  7.32 us

profile of v3, /device:TPU:0, one launch (start us, length us, event | category | flops | bytes accessed | tf_op | source)
XLA Modules:
  0.0 37.9 jit_solution(9793794282569840152)
XLA Ops:
  0.6 30.0 %krylov.1 = (f32[192,1024]{1,0:T(8,128)}, f32[8,16,128]{2,1,0:T(8,128)}) custom-call(f32[6,8]{1,0:T(8,128)} %table_hbm.1, s32[8,128]{1,0:T(8,128)} %bitcast.12, s32[2,64]{1,0:T(2,128)} %electrodes_hbm.1, f32[512,128]{1,0:T(8,128)} %bitcast.9), custom_call_target="tpu_custom_call" | custom-call | tf_op jit(solution)/shard_map/krylov/pallas_call | solution.py:837
  30.6 7.3 %combine.1 = (f32[512,128]{1,0:T(8,128)}, f32[512,128]{1,0:T(8,128)}) custom-call(f32[128,128]{1,0:T(8,128)} %bitcast.11, f32[192,1024]{1,0:T(8,128)} %get-tuple-element.7.base_hbm, f32[512,128]{1,0:T(8,128)} %bitcast.10), custom_call_target="tpu_custom_call" | custom-call | tf_op jit(solution)/shard_map/combine/pallas_call | solution.py:838
